TPU v7x, 32 devices: a whole 2x2x4 slice. The times are simulated.
32 devices in a mesh: rep: 4 (over y, core), fsdp: 8 (over z, x).
Axes of the slice: x: 2, y: 2, z: 4, core: 2. Of those that a mesh axis runs over, the one named last changes fastest.
Arguments:
- patches: bfloat16 [384, 80, 768], P(('rep', 'fsdp')), may hold values from -6 to 6
- visible_count: int32 [384], P(('rep', 'fsdp')), may hold values from 20 to 78, as said below
- patch_index: int32 [384, 80], P(('rep', 'fsdp')), may hold values from 0 to 195, as said below
- prenorm_gain: bfloat16 [768], P('fsdp'), may hold values from 0.5 to 1.5
- prenorm_bias: bfloat16 [768], P('fsdp'), may hold values from -4 to 4
- heads_weight: bfloat16 [768, 2304], P('fsdp'), may hold values from -0.21875 to 0.21875
- heads_bias: bfloat16 [1536], P('fsdp'), may hold values from -4 to 4
- output_weight: bfloat16 [768, 768], P('fsdp'), may hold values from -0.625 to 0.625
- output_bias: bfloat16 [768], P('fsdp'), may hold values from -4 to 4
- midnorm_gain: bfloat16 [768], P('fsdp'), may hold values from 0.5 to 1.5
- midnorm_bias: bfloat16 [768], P('fsdp'), may hold values from -4 to 4
- expand_weight: bfloat16 [768, 3072], P('fsdp'), may hold values from -0.21875 to 0.21875
- expand_bias: bfloat16 [3072], P('fsdp'), may hold values from -4 to 4
- reduce_weight: bfloat16 [3072, 768], P('fsdp'), may hold values from -0.109375 to 0.109375
- reduce_bias: bfloat16 [768], P('fsdp'), may hold values from -4 to 4
- upstream: bfloat16 [384, 80, 768], P(('rep', 'fsdp')), may hold values from -6 to 6
Outputs:
- block_result_output: bfloat16 [384, 80, 768], P(('rep', 'fsdp'))
- patches_grad: bfloat16 [384, 80, 768], P(('rep', 'fsdp'))
- prenorm_gain_grad: float32 [768], P('fsdp')
- prenorm_bias_grad: float32 [768], P('fsdp')
- heads_weight_grad: float32 [768, 2304], P('fsdp')
- head_bias_gradient: float32 [1536], P('fsdp')
- output_weight_grad: float32 [768, 768], P('fsdp')
- output_bias_grad: float32 [768], P('fsdp')
- midnorm_gain_grad: float32 [768], P('fsdp')
- midnorm_bias_grad: float32 [768], P('fsdp')
- expand_weight_grad: float32 [768, 3072], P('fsdp')
- expand_bias_grad: float32 [3072], P('fsdp')
- reduce_weight_grad: float32 [3072, 768], P('fsdp')
- reduce_bias_grad: float32 [768], P('fsdp')
Inputs may be any that keep to these rules, and one draw needn't show every extreme that they name: `visible_count`: visible patches of each image; slots from this count on are padding. `patch_index`: the slots of one image hold distinct patches.
All inputs are finite; a program needn't handle non-finite values.
Results may differ from a plain program's by a relative error of at most 0.013.
Values may be sent and summed in bfloat16 or wider, within the bound.
No kernel may reach another device: no remote copies, remote signals or barrier semaphores. Data moves between devices by JAX's collectives and lax.ppermute only.
A program may use at most 192 MiB of HBM per device.

v0:
```python
import jax
import jax.numpy as jnp
from jax import lax
from jax.sharding import PartitionSpec as P

D = 768
HEADS = 12
HEAD_DIM = 64
SLOTS = 80
GRID = 14


epsilon = 1e-06
masked_score = -1e30


def position_table(patch_ids):
    quarter = D // 4
    frequency = 1.0 / 10000.0 ** (jnp.arange(quarter, dtype=jnp.float32) / quarter)
    row_place = (patch_ids // GRID).astype(jnp.float32)[..., None] * frequency
    col_place = (patch_ids % GRID).astype(jnp.float32)[..., None] * frequency
    return jnp.concatenate(
        [jnp.sin(row_place), jnp.cos(row_place), jnp.sin(col_place), jnp.cos(col_place)], axis=-1
    )


def layer_core(values, norm_gain):
    center = values - jnp.mean(values, axis=-1, keepdims=True)
    spread = jnp.mean(center * center, axis=-1, keepdims=True)
    return center * lax.rsqrt(spread + epsilon) * norm_gain


def gelu_gate_value(values):
    return jax.nn.gelu(values, approximate=False)


def attention_scores(queries, keys_all, key_padding_mask):
    scores = jnp.einsum(
        "bqhd,bkhd->bhqk", queries, keys_all, preferred_element_type=jnp.float32
    ) * HEAD_DIM ** (-0.5)
    return jnp.where(key_padding_mask[:, None, None, :], scores, masked_score)


def column_sum(values):
    return jnp.sum(values.astype(jnp.float32), axis=0)


def body(
    patches,
    visible_count,
    patch_index,
    prenorm_gain,
    prenorm_bias,
    heads_weight,
    heads_bias,
    output_weight,
    output_bias,
    midnorm_gain,
    midnorm_bias,
    expand_weight,
    expand_bias,
    reduce_weight,
    reduce_bias,
    upstream,
):
    count_img = patches.shape[0]
    (
        pre_gain,
        pre_shift,
        heads_full,
        heads_bias_full,
        out_full,
        out_bias_full,
        mid_gain,
        mid_shift,
        expand_full,
        expand_bias_full,
        reduce_full,
        reduce_bias_full,
    ) = (
        lax.all_gather(prenorm_gain, "fsdp", axis=0, tiled=True),
        lax.all_gather(prenorm_bias, "fsdp", axis=0, tiled=True),
        lax.all_gather(heads_weight, "fsdp", axis=0, tiled=True),
        lax.all_gather(heads_bias, "fsdp", axis=0, tiled=True),
        lax.all_gather(output_weight, "fsdp", axis=0, tiled=True),
        lax.all_gather(output_bias, "fsdp", axis=0, tiled=True),
        lax.all_gather(midnorm_gain, "fsdp", axis=0, tiled=True),
        lax.all_gather(midnorm_bias, "fsdp", axis=0, tiled=True),
        lax.all_gather(expand_weight, "fsdp", axis=0, tiled=True),
        lax.all_gather(expand_bias, "fsdp", axis=0, tiled=True),
        lax.all_gather(reduce_weight, "fsdp", axis=0, tiled=True),
        lax.all_gather(reduce_bias, "fsdp", axis=0, tiled=True),
    )
    slot_index_list = jnp.arange(SLOTS, dtype=jnp.int32)
    key_padding_mask = slot_index_list[None, :] < visible_count[:, None]
    start = (patches.astype(jnp.float32) + position_table(patch_index)).reshape(-1, D)
    first = (
        layer_core(start, pre_gain.astype(jnp.float32)) + pre_shift.astype(jnp.float32)
    ).astype(jnp.bfloat16)
    bias_full = jnp.concatenate(
        [
            heads_bias_full[:D].astype(jnp.float32),
            jnp.zeros((D,), jnp.float32),
            heads_bias_full[D:].astype(jnp.float32),
        ]
    )
    projected = (jnp.dot(first, heads_full, preferred_element_type=jnp.float32) + bias_full).astype(
        jnp.bfloat16
    )
    projected = projected.reshape(count_img, SLOTS, 3, HEADS, HEAD_DIM)
    queries = projected[:, :, 0]
    keys_all = projected[:, :, 1]
    values_all = projected[:, :, 2]
    masked = attention_scores(queries, keys_all, key_padding_mask)
    row_peak = jnp.max(masked, axis=-1, keepdims=True)
    raised = jnp.exp(masked - row_peak)
    row_total = jnp.sum(raised, axis=-1, keepdims=True)
    attend = (raised / row_total).astype(jnp.bfloat16)
    log_total = row_peak + jnp.log(row_total)
    mixed = (
        jnp.einsum("bhqk,bkhd->bqhd", attend, values_all, preferred_element_type=jnp.float32)
        .astype(jnp.bfloat16)
        .reshape(-1, D)
    )
    branch = jnp.dot(mixed, out_full, preferred_element_type=jnp.float32) + out_bias_full.astype(
        jnp.float32
    )
    middle = start + branch
    second = (
        layer_core(middle, mid_gain.astype(jnp.float32)) + mid_shift.astype(jnp.float32)
    ).astype(jnp.bfloat16)
    hidden = jnp.dot(
        second, expand_full, preferred_element_type=jnp.float32
    ) + expand_bias_full.astype(jnp.float32)
    active = gelu_gate_value(hidden).astype(jnp.bfloat16)
    result = (
        middle
        + jnp.dot(active, reduce_full, preferred_element_type=jnp.float32)
        + reduce_bias_full.astype(jnp.float32)
    )
    block_result_output = result.astype(jnp.bfloat16).reshape(count_img, SLOTS, D)
    heads_back, out_back, expand_back, reduce_back, pre_gain_back, mid_gain_back = (
        lax.all_gather(heads_weight, "fsdp", axis=0, tiled=True),
        lax.all_gather(output_weight, "fsdp", axis=0, tiled=True),
        lax.all_gather(expand_weight, "fsdp", axis=0, tiled=True),
        lax.all_gather(reduce_weight, "fsdp", axis=0, tiled=True),
        lax.all_gather(prenorm_gain, "fsdp", axis=0, tiled=True),
        lax.all_gather(midnorm_gain, "fsdp", axis=0, tiled=True),
    )
    seed = (upstream * key_padding_mask[:, :, None].astype(jnp.bfloat16)).reshape(-1, D)
    grad_reduce = jnp.dot(active.T, seed, preferred_element_type=jnp.float32)
    reduce_bias_gradient_sum = column_sum(seed)
    d_active = jnp.dot(seed, reduce_back.T, preferred_element_type=jnp.float32)
    gate_value, gate_pull = jax.vjp(gelu_gate_value, hidden)
    d_hidden = gate_pull(d_active)[0].astype(jnp.bfloat16)
    grad_expand = jnp.dot(second.T, d_hidden, preferred_element_type=jnp.float32)
    grad_expbias = column_sum(d_hidden)
    d_second = jnp.dot(d_hidden, expand_back.T, preferred_element_type=jnp.float32)
    mid_value, mid_pull = jax.vjp(layer_core, middle, mid_gain_back.astype(jnp.float32))
    d_middle_norm, grad_midgain = mid_pull(d_second)
    grad_midshift = jnp.sum(d_second, axis=0)
    d_middle = seed.astype(jnp.float32) + d_middle_norm
    d_branch = d_middle.astype(jnp.bfloat16)
    grad_outproj = jnp.dot(mixed.T, d_branch, preferred_element_type=jnp.float32)
    grad_outbias = column_sum(d_branch)
    d_mixed = jnp.dot(d_branch, out_back.T, preferred_element_type=jnp.float32).astype(jnp.bfloat16)
    d_mixed = d_mixed.reshape(count_img, SLOTS, HEADS, HEAD_DIM)
    masked_again = attention_scores(queries, keys_all, key_padding_mask)
    probs_back = jnp.exp(masked_again - log_total)
    attend_again = probs_back.astype(jnp.bfloat16)
    d_values = jnp.einsum(
        "bhqk,bqhd->bkhd", attend_again, d_mixed, preferred_element_type=jnp.float32
    )
    d_attend = jnp.einsum(
        "bqhd,bkhd->bhqk", d_mixed, values_all, preferred_element_type=jnp.float32
    )
    d_scores = (
        probs_back * (d_attend - jnp.sum(probs_back * d_attend, axis=-1, keepdims=True))
    ).astype(jnp.bfloat16)
    d_queries = jnp.einsum(
        "bhqk,bkhd->bqhd", d_scores, keys_all, preferred_element_type=jnp.float32
    ) * HEAD_DIM ** (-0.5)
    d_keys = jnp.einsum(
        "bhqk,bqhd->bkhd", d_scores, queries, preferred_element_type=jnp.float32
    ) * HEAD_DIM ** (-0.5)
    d_projected = (
        jnp.stack([d_queries, d_keys, d_values], axis=2).astype(jnp.bfloat16).reshape(-1, 3 * D)
    )
    grad_inproj = jnp.dot(first.T, d_projected, preferred_element_type=jnp.float32)
    grad_inbias = jnp.concatenate(
        [column_sum(d_projected[:, :D]), column_sum(d_projected[:, 2 * D :])]
    )
    first_layer_gradient = jnp.dot(d_projected, heads_back.T, preferred_element_type=jnp.float32)
    pre_value, pre_pull = jax.vjp(layer_core, start, pre_gain_back.astype(jnp.float32))
    d_start_norm, grad_pregain = pre_pull(first_layer_gradient)
    prenorm_shift_gradient = jnp.sum(first_layer_gradient, axis=0)
    patches_grad = (d_middle + d_start_norm).astype(jnp.bfloat16).reshape(count_img, SLOTS, D)
    shares = (
        lax.psum_scatter(grad_pregain, "fsdp", scatter_dimension=0, tiled=True),
        lax.psum_scatter(prenorm_shift_gradient, "fsdp", scatter_dimension=0, tiled=True),
        lax.psum_scatter(grad_inproj, "fsdp", scatter_dimension=0, tiled=True),
        lax.psum_scatter(grad_inbias, "fsdp", scatter_dimension=0, tiled=True),
        lax.psum_scatter(grad_outproj, "fsdp", scatter_dimension=0, tiled=True),
        lax.psum_scatter(grad_outbias, "fsdp", scatter_dimension=0, tiled=True),
        lax.psum_scatter(grad_midgain, "fsdp", scatter_dimension=0, tiled=True),
        lax.psum_scatter(grad_midshift, "fsdp", scatter_dimension=0, tiled=True),
        lax.psum_scatter(grad_expand, "fsdp", scatter_dimension=0, tiled=True),
        lax.psum_scatter(grad_expbias, "fsdp", scatter_dimension=0, tiled=True),
        lax.psum_scatter(grad_reduce, "fsdp", scatter_dimension=0, tiled=True),
        lax.psum_scatter(reduce_bias_gradient_sum, "fsdp", scatter_dimension=0, tiled=True),
    )
    finals = (
        lax.psum(shares[0].astype(jnp.bfloat16), "rep").astype(jnp.float32),
        lax.psum(shares[1].astype(jnp.bfloat16), "rep").astype(jnp.float32),
        lax.psum(shares[2].astype(jnp.bfloat16), "rep").astype(jnp.float32),
        lax.psum(shares[3].astype(jnp.bfloat16), "rep").astype(jnp.float32),
        lax.psum(shares[4].astype(jnp.bfloat16), "rep").astype(jnp.float32),
        lax.psum(shares[5].astype(jnp.bfloat16), "rep").astype(jnp.float32),
        lax.psum(shares[6].astype(jnp.bfloat16), "rep").astype(jnp.float32),
        lax.psum(shares[7].astype(jnp.bfloat16), "rep").astype(jnp.float32),
        lax.psum(shares[8].astype(jnp.bfloat16), "rep").astype(jnp.float32),
        lax.psum(shares[9].astype(jnp.bfloat16), "rep").astype(jnp.float32),
        lax.psum(shares[10].astype(jnp.bfloat16), "rep").astype(jnp.float32),
        lax.psum(shares[11].astype(jnp.bfloat16), "rep").astype(jnp.float32),
    )
    return (
        block_result_output,
        patches_grad,
        finals[0],
        finals[1],
        finals[2],
        finals[3],
        finals[4],
        finals[5],
        finals[6],
        finals[7],
        finals[8],
        finals[9],
        finals[10],
        finals[11],
    )


def solution(mesh):
    return jax.shard_map(
        body,
        mesh=mesh,
        in_specs=(
            P(("rep", "fsdp"), None, None),
            P(("rep", "fsdp")),
            P(("rep", "fsdp"), None),
            P("fsdp"),
            P("fsdp"),
            P("fsdp", None),
            P("fsdp"),
            P("fsdp", None),
            P("fsdp"),
            P("fsdp"),
            P("fsdp"),
            P("fsdp", None),
            P("fsdp"),
            P("fsdp", None),
            P("fsdp"),
            P(("rep", "fsdp"), None, None),
        ),
        out_specs=(
            P(("rep", "fsdp"), None, None),
            P(("rep", "fsdp"), None, None),
            P("fsdp"),
            P("fsdp"),
            P("fsdp", None),
            P("fsdp"),
            P("fsdp", None),
            P("fsdp"),
            P("fsdp"),
            P("fsdp"),
            P("fsdp", None),
            P("fsdp"),
            P("fsdp", None),
            P("fsdp"),
        ),
        check_vma=False,
    )
```

profile of v0, /device:TPU:0, one launch (start us, length us, event | category | flops | bytes accessed | tf_op | source)
XLA Modules:
  0.0 931.3 jit_solution(14372484546486761478)
XLA Ops:
  19.2 40.1 %all-reduce.16 = (bf16[1536]{0:T(1024)(128)(2,1)S(1)}, bf16[768]{0:T(1024)(128)(2,1)S(1)}, bf16[768]{0:T(1024)(128)(2,1)S(1)}, bf16[768]{0:T(1024)(128)(2,1)S(1)...) all-reduce(bf16[1536]{0:T(1024)(128)(2,1)S(1)} %dynamic-update-slic, ...), channel_id=1, replica_groups=mesh['rep'=4,'fsdp'=8] {'fsdp'}, use_global_device_ids=true, to_apply=%add.2 | all-reduce | flops 6144 | bytes 24576
  59.3 26.2 %all-gather = bf16[8,1,384]{2,1,0:T(2,128)(2,1)S(1)} all-gather(bf16[1,1,384]{2,1,0:T(2,128)(2,1)S(1)} %reshape.244), channel_id=1, replica_groups=mesh['rep'=4,'fsdp'=8] {'fsdp'}, dimensions={0}, use_global_device_ids=true | all-gather | bytes 6912 | tf_op jit(solution)/shard_map/all_gather | solution.py:90
  86.2 6.9 multiply_sine_fusion.1
  96.0 3.5 convert_reduce_fusion.3
  99.5 8.0 add_convert_fusion.1
  107.5 14.2 %reshape.269 = bf16[12,80,3,12,64]{4,3,2,1,0:T(8,128)(2,1)} reshape(bf16[960,2304]{1,0:T(8,128)(2,1)} %add_convert_fusion.1) | data formatting | bytes 8847360 | tf_op jit(solution)/shard_map/reshape | solution.py:110
  121.7 8.4 fusion.47
  130.1 5.3 copy.73
  135.4 5.3 copy.74
  140.7 5.3 copy.75
  146.0 4.5 fusion.49
  155.1 3.5 copy.57
  158.6 5.8 reshape.218
  164.4 3.3 fusion.50
  169.8 31.7 %all-gather.10.cloned.1.call-done = bf16[768,3072]{1,0:T(8,128)(2,1)} async-done(((bf16[96,3072]{1,0:T(8,128)(2,1)}), bf16[768,3072]{1,0:T(8,128)(2,1)}) %all-gather.10.cloned.1.call-update) | async-done | bytes 4718608 | tf_op jit(solution)/shard_map/all_gather | solution.py:89
  201.6 12.4 %fusion.42 = f32[960,3072]{1,0:T(8,128)} fusion(bf16[768,3072]{1,0:T(8,128)(2,1)} %all-gather.10.cloned.1.call-done, f32[960,768]{1,0:T(8,128)} %copy-done.4, f32[768]{0:T(1024)S(1)} %convert_element_type.212, f32[768]{0:T(1024)S(1)} %convert_element_type.211, f32[960]{0:T(1024)S(1)} %fusion.38, f32[960]{0:T(1024)S(1)} %broadcast_multiply_fusion.2), kind=kOutput, calls=%fused_computation.109 | convolution fusion | flops 4533534720 | bytes 19478016 | tf_op jit(solution)/shard_map/dot_general | solution.py:132
  214.0 67.7 %all-gather.12.cloned.1.call-done = bf16[3072,768]{1,0:T(8,128)(2,1)} async-done(((bf16[384,768]{1,0:T(8,128)(2,1)}), bf16[3072,768]{1,0:T(8,128)(2,1)}) %all-gather.12.cloned.1.call-update) | async-done | bytes 4718608 | tf_op jit(solution)/shard_map/all_gather | solution.py:91
  281.7 36.1 %convert_reduce_fusion = (f32[3072]{0:T(1024)S(1)}, bf16[960,3072]{1,0:T(8,128)(2,1)S(1)}, f32[960,3072]{1,0:T(8,128)}) fusion(f32[960,3072]{1,0:T(8,128)} %fusion.42, f32[3072]{0:T(1024)S(1)} %bitcast.93, bf16[960,768]{1,0:T(8,128)(2,1)S(1)} %bitcast.89, bf16[3072,768]{1,0:T(8,128)(2,1)} %all-gather.12.cloned.1.call-done), kind=kOutput, calls=%fused_computation.3 | convolution fusion | flops 4751029248 | bytes 35708928 | tf_op jit(solution)/shard_map/dot_general | solution.py:153
  317.9 5.2 multiply_reduce_fusion.1
  326.9 2.8 fusion.52
  333.4 4.5 reshape.270
  337.9 5.4 copy.59
  343.2 6.3 multiply_reduce_fusion
  349.5 1.9 multiply_convert_fusion.1
  356.5 4.1 maximum_convert_fusion
  360.6 18.3 %copy.64 = bf16[12,80,3,12,64]{1,0,4,3,2:T(8,128)(2,1)} copy(bf16[12,80,3,12,64]{1,4,3,0,2:T(8,128)(2,1)} %maximum_convert_fusion) | data formatting | bytes 8847360 | tf_op jit(solution)/shard_map/convert_element_type | solution.py:187
  379.0 14.2 %convert_element_type.226 = bf16[960,2304]{0,1:T(8,128)(2,1)} reshape(bf16[12,80,3,12,64]{1,0,4,3,2:T(8,128)(2,1)} %copy.64) | data formatting | bytes 8847360 | tf_op jit(solution)/shard_map/convert_element_type | solution.py:187
  393.1 8.3 fusion.51
  403.2 10.5 %fusion.41 = f32[768,3072]{1,0:T(8,128)} fusion(bf16[960,3072]{1,0:T(8,128)(2,1)} %copy-done.16, f32[960,768]{1,0:T(8,128)S(1)} %copy-done.6, f32[768]{0:T(1024)S(1)} %copy-done.38, f32[768]{0:T(1024)S(1)} %copy-done.36, f32[960]{0:T(1024)S(1)} %copy-done.32, f32[960]{0:T(1024)S(1)} %copy-done.30), kind=kOutput, calls=%fused_computation.108 | convolution fusion | flops 4533534720 | bytes 18298368 | tf_op jit(solution)/shard_map/dot_general | solution.py:156
  413.8 9.3 %multiply_convert_fusion = bf16[960,3072]{1,0:T(8,128)(2,1)S(1)} fusion(f32[960,3072]{1,0:T(8,128)} %get-tuple-element.53, f32[960,3072]{1,0:T(8,128)} %fusion.42, f32[3072]{0:T(1024)S(1)} %bitcast.94), kind=kLoop, calls=%fused_computation.5 | loop fusion | flops 11796480 | bytes 29503488 | tf_op jit(solution)/shard_map/convert_element_type | solution.py:135
  423.2 2.5 copy-done.17
  425.7 7.7 fusion.53
  435.9 8.5 multiply_reduce_fusion.2
  444.4 2.4 add_add_fusion
  446.8 2.3 copy-done.18
  449.1 8.2 add_convert_fusion.4
  458.9 69.9 %reduce-scatter.5.cloned.1.call-done = f32[96,2304]{1,0:T(8,128)} async-done(((f32[768,2304]{1,0:T(8,128)}), f32[96,2304]{1,0:T(8,128)}) %reduce-scatter.5.cloned.1.call-update) | async-done | bytes 884752 | tf_op jit(solution)/shard_map/reduce_scatter | solution.py:201
  528.8 2.0 convert_element_type.234
  530.8 164.4 %reduce-scatter.9.cloned.1.call-done = f32[96,3072]{1,0:T(8,128)} async-done(((f32[768,3072]{1,0:T(8,128)}), f32[96,3072]{1,0:T(8,128)}) %reduce-scatter.9.cloned.1.call-update) | async-done | bytes 1179664 | tf_op jit(solution)/shard_map/reduce_scatter | solution.py:207
  695.2 2.2 convert_element_type.249
  697.4 164.3 %reduce-scatter.11.cloned.1.call-done = f32[384,768]{1,0:T(8,128)} async-done(((f32[3072,768]{1,0:T(8,128)}), f32[384,768]{1,0:T(8,128)}) %reduce-scatter.11.cloned.1.call-update) | async-done | bytes 1179664 | tf_op jit(solution)/shard_map/reduce_scatter | solution.py:209
  861.7 2.1 convert_element_type.254
  863.9 2.4 convert_reduce_fusion.2
  866.5 35.6 %all-reduce.15 = (bf16[768]{0:T(1024)(128)(2,1)S(1)}, bf16[768]{0:T(1024)(128)(2,1)S(1)}, bf16[1536]{0:T(1024)(128)(2,1)S(1)}, bf16[768]{0:T(1024)(128)(2,1)S(1)...) all-reduce(f32[768]{0:T(1024)S(1)} %get-tuple-element.18, ...), channel_id=2, replica_groups=mesh['rep'=4,'fsdp'=8] {'fsdp'}, use_global_device_ids=true, to_apply=%region_12.13.clone | all-reduce | flops 9216 | bytes 55296
  902.7 6.4 all-reduce.17
  913.4 4.0 add_convert_fusion.3
  919.0 2.0 convert_element_type.235
  921.0 2.2 convert_element_type.250
  (213 shorter events, 44.9 us)
Async XLA Ops:
  7.2 92.3 %all-gather.6.cloned.1.call-start = ((), (), s32[]{:S(2)}) async-start(), calls=%async_computation.4 | async-start | bytes 3981312 | tf_op jit(solution)/shard_map/all_gather | solution.py:83
  7.9 156.4 %all-gather.8.cloned.1.call-start = ((), (), s32[]{:S(2)}) async-start(), calls=%async_computation.5 | async-start | bytes 1327104 | tf_op jit(solution)/shard_map/all_gather | solution.py:85
  8.7 192.9 %all-gather.10.cloned.1.call-start = ((), (), s32[]{:S(2)}) async-start(), calls=%async_computation.6 | async-start | bytes 5308416 | tf_op jit(solution)/shard_map/all_gather | solution.py:89
  9.4 272.3 %all-gather.12.cloned.1.call-start = ((), (), s32[]{:S(2)}) async-start(), calls=%async_computation.7 | async-start | bytes 5308416 | tf_op jit(solution)/shard_map/all_gather | solution.py:91
  10.0 447.3 %reduce-scatter.7.cloned.1.call-start = ((), (), s32[]{:S(2)}) async-start(), calls=%async_computation.9 | async-start | bytes 2654208 | tf_op jit(solution)/shard_map/reduce_scatter | solution.py:203
  59.2 33.9 %copy-start.20 = (bf16[12,80,768]{2,1,0:T(8,128)(2,1)S(1)}, bf16[12,80,768]{2,1,0:T(8,128)(2,1)}, u32[]{:S(2)}) copy-start(bf16[12,80,768]{2,1,0:T(8,128)(2,1)} %param.16) | copy-start | bytes 4423684
  59.2 40.3 %copy-start.43 = (f32[768]{0:T(1024)}, f32[768]{0:T(1024)S(1)}, u32[]{:S(2)}) copy-start(f32[768]{0:T(1024)S(1)} %convert_element_type.201) | copy-start | bytes 9220
  59.3 142.3 %copy-start.35 = (f32[768]{0:T(1024)}, f32[768]{0:T(1024)S(1)}, u32[]{:S(2)}) copy-start(f32[768]{0:T(1024)S(1)} %convert_element_type.211) | copy-start | bytes 9220
  59.3 40.2 %copy-start.51 = (f32[768]{0:T(1024)}, f32[768]{0:T(1024)S(1)}, u32[]{:S(2)}) copy-start(f32[768]{0:T(1024)S(1)} %convert_element_type.202) | copy-start | bytes 9220
  59.3 142.3 %copy-start.37 = (f32[768]{0:T(1024)}, f32[768]{0:T(1024)S(1)}, u32[]{:S(2)}) copy-start(f32[768]{0:T(1024)S(1)} %convert_element_type.212) | copy-start | bytes 9220
  94.2 70.2 %copy-start.1 = (f32[12,80,768]{2,1,0:T(8,128)}, f32[12,80,768]{2,1,0:T(8,128)S(1)}, u32[]{:S(2)}) copy-start(f32[12,80,768]{2,1,0:T(8,128)S(1)} %get-tuple-element.59) | copy-start | bytes 8847364
  94.2 5.3 copy-start.33
  94.3 5.2 copy-start.46
  95.8 11.7 %copy-start.41 = (f32[960]{0:T(1024)}, f32[960]{0:T(1024)S(1)}, u32[]{:S(2)}) copy-start(f32[960]{0:T(1024)S(1)} %add.160) | copy-start | bytes 11524
  95.9 11.7 %copy-start.48 = (f32[960]{0:T(1024)}, f32[960]{0:T(1024)S(1)}, u32[]{:S(2)}) copy-start(f32[960]{0:T(1024)S(1)} %rsqrt.25) | copy-start | bytes 11524
  150.5 2.8 copy-start
  150.5 2.9 copy-start.24
  150.5 3.4 copy-start.15
  167.7 46.2 %copy-start.29 = (f32[960]{0:T(1024)}, f32[960]{0:T(1024)S(1)}, u32[]{:S(2)}) copy-start(f32[960]{0:T(1024)S(1)} %broadcast_multiply_fusion.2) | copy-start | bytes 11524
  169.8 44.1 %copy-start.39 = (f32[960]{0:T(1024)}, f32[960]{0:T(1024)S(1)}, u32[]{:S(2)}) copy-start(f32[960]{0:T(1024)S(1)} %multiply_reduce_fusion.5) | copy-start | bytes 11524
  169.8 44.1 %copy-start.31 = (f32[960]{0:T(1024)}, f32[960]{0:T(1024)S(1)}, u32[]{:S(2)}) copy-start(f32[960]{0:T(1024)S(1)} %fusion.38) | copy-start | bytes 11524
  169.8 111.8 %copy-start.13 = (bf16[12,80,768]{2,1,0:T(8,128)(2,1)S(1)}, bf16[12,80,768]{2,1,0:T(8,128)(2,1)}, u32[]{:S(2)}) copy-start(bf16[12,80,768]{2,1,0:T(8,128)(2,1)} %get-tuple-element.50) | copy-start | bytes 4423684
  281.7 36.1 %copy-start.5 = (f32[960,768]{1,0:T(8,128)S(1)}, f32[960,768]{1,0:T(8,128)}, u32[]{:S(2)}) copy-start(f32[960,768]{1,0:T(8,128)} %copy-done.4) | copy-start | bytes 8847364
  281.7 36.1 %copy-start.30 = (f32[960]{0:T(1024)S(1)}, f32[960]{0:T(1024)}, u32[]{:S(2)}) copy-start(f32[960]{0:T(1024)} %copy-done.29) | copy-start | bytes 11524
  281.7 36.2 %copy-start.32 = (f32[960]{0:T(1024)S(1)}, f32[960]{0:T(1024)}, u32[]{:S(2)}) copy-start(f32[960]{0:T(1024)} %copy-done.31) | copy-start | bytes 11524
  281.7 36.2 %copy-start.36 = (f32[768]{0:T(1024)S(1)}, f32[768]{0:T(1024)}, u32[]{:S(2)}) copy-start(f32[768]{0:T(1024)} %copy-done.35) | copy-start | bytes 9220
  281.7 36.2 %copy-start.55 = (bf16[768,3072]{1,0:T(8,128)(2,1)S(1)}, bf16[768,3072]{1,0:T(8,128)(2,1)}, u32[]{:S(2)}) copy-start(bf16[768,3072]{1,0:T(8,128)(2,1)} %all-gather.10.cloned.1.call-done) | copy-start | bytes 14155780
  317.8 5.3 copy-start.16
  317.8 5.3 copy-start.40
  324.2 2.7 copy-start.19
  326.9 3.0 copy-start.2
  326.9 3.0 copy-start.34
  326.9 3.0 copy-start.44
  326.9 3.0 copy-start.45
  326.9 3.0 copy-start.52
  329.7 199.1 %reduce-scatter.5.cloned.1.call-start = ((), (), s32[]{:S(2)}) async-start(), calls=%async_computation.8 | async-start | bytes 7962624 | tf_op jit(solution)/shard_map/reduce_scatter | solution.py:201
  337.8 11.7 %slice-start = ((s8[5898240]{0:T(1024)(128)(4,1)}), s8[1703936]{0:T(1024)(128)(4,1)S(1)}, s32[]{:S(2)}) async-start(s8[5898240]{0:T(1024)(128)(4,1)} %bitcast.84), calls=%async_computation.13 | async-start | bytes 3407872
  343.2 6.3 slice-start.1
  379.0 14.2 %copy-start.21 = (bf16[12,80,768]{2,1,0:T(8,128)(2,1)S(1)}, bf16[12,80,768]{2,1,0:T(8,128)(2,1)}, u32[]{:S(2)}) copy-start(bf16[12,80,768]{2,1,0:T(8,128)(2,1)} %add_convert_fusion.2) | copy-start | bytes 4423684
  401.4 293.8 %reduce-scatter.9.cloned.1.call-start = ((), (), s32[]{:S(2)}) async-start(), calls=%async_computation.10 | async-start | bytes 10616832 | tf_op jit(solution)/shard_map/reduce_scatter | solution.py:207
  413.8 447.9 %reduce-scatter.11.cloned.1.call-start = ((), (), s32[]{:S(2)}) async-start(), calls=%async_computation.11 | async-start | bytes 10616832 | tf_op jit(solution)/shard_map/reduce_scatter | solution.py:209
  413.8 11.9 %copy-start.14 = (bf16[12,80,768]{2,1,0:T(8,128)(2,1)S(1)}, bf16[12,80,768]{2,1,0:T(8,128)(2,1)}, u32[]{:S(2)}) copy-start(bf16[12,80,768]{2,1,0:T(8,128)(2,1)} %get-tuple-element.50) | copy-start | bytes 4423684
  433.4 484.0 %all-reduce.21.cloned.1.call-start = ((), (), s32[]{:S(2)}) async-start(), calls=%async_computation.12 | async-start | bytes 3538944 | tf_op jit(solution)/shard_map/psum | solution.py:215
  435.8 8.5 copy-start.42
  444.4 4.7 copy-start.18
  697.4 168.9 %copy-start.8 = (f32[960,768]{1,0:T(8,128)S(1)}, f32[960,768]{1,0:T(8,128)}, u32[]{:S(2)}) copy-start(f32[960,768]{1,0:T(8,128)} %add_add_fusion) | copy-start | bytes 8847364
  863.8 2.6 copy-start.50
  917.3 5.9 copy-start.26
  (20 other events, 38.4 us)
Sparse Core Ops, SparseCore 0:
  10.2 68.4 all-gather.5
  80.9 39.7 all-gather.7
  122.9 78.6 all-gather.9
  203.6 78.0 all-gather.11
  329.9 67.1 reduce-scatter.6
  401.6 127.2 reduce-scatter.4
  532.8 162.3 reduce-scatter.8
  699.2 162.4 reduce-scatter.10
  865.6 45.9 all-reduce.20
where the time goes:
time: 942 us; the launch traced here: 931 us
  waiting for transfers between devices  501 us (53%)
  matrix products  128 us (14%)
  local copies, waits for them, and re-layouts  112 us (12%)
  blocking collectives  108 us (11%)
  other arithmetic  62.7 us (7%)
  between operations  18.5 us (2%)
    reduce_scatter x1, waiting for transfers between devices, body(): lax.psum_scatter(grad_expand, 'fsdp', scatter_dimension=0, tiled=True)  164 us
    reduce_scatter x1, waiting for transfers between devices, body(): lax.psum_scatter(grad_reduce, 'fsdp', scatter_dimension=0, tiled=True)  164 us
    unnamed x2, blocking collectives  75.7 us
    reduce_scatter x1, waiting for transfers between devices, body(): lax.psum_scatter(grad_inproj, 'fsdp', scatter_dimension=0, tiled=True)  69.9 us
    all_gather x1, waiting for transfers between devices, body(): lax.all_gather(reduce_weight, 'fsdp', axis=0, tiled=True)  67.7 us
    unnamed x145, local copies, waits for them, and re-layouts  37.7 us
    dot_general x1, matrix products, body(): d_active = jnp.dot(seed, reduce_back.T, preferred_element_type=jnp.float32)  36.1 us
    convert_element_type x2, local copies, waits for them, and re-layouts, body(): jnp.stack([d_queries, d_keys, d_values], axis=2).astype(jnp.bfloat16)  32.5 us
  transfers between devices with their start and end apart: 9, of which 5 were waited for; matrix products, arithmetic and copies ran while one was open for 25% of the time, Pallas kernels for 0%

commit v1 on v0

v1 whole, which is shorter than its diff:
```python
import functools

import numpy as np
import jax
import jax.numpy as jnp
from jax import lax
from jax.experimental import pallas as pl
from jax.experimental.pallas import tpu as pltpu
from jax.sharding import PartitionSpec as P

D = 768
FF = 3072
HEADS = 12
HEAD_DIM = 64
SLOTS = 80
GRID = 14
NF = 8
RB = D // NF
FB = FF // NF
CH = 3
CW = FF // CH
LANE = 128
HB = 3 * D // LANE
OB = D // LANE
EB = CW // LANE
QH = HB * RB // 4
QO = OB * RB // 4
QM = (EB * RB + OB * LANE) // 4
SM = 16

EPS = 1e-06
NEG = -1e30
bf16 = jnp.bfloat16
f32 = jnp.float32
NN = (((1,), (0,)), ((), ()))
NT = (((1,), (1,)), ((), ()))
TN = (((0,), (0,)), ((), ()))
VMEM_LIMIT = 60 << 20


def mm(a, b, dims):
    return lax.dot_general(a, b, dims, preferred_element_type=f32)


def params(limit=VMEM_LIMIT):
    return pltpu.CompilerParams(vmem_limit_bytes=limit)


def whole(shape):
    return pl.BlockSpec(shape, lambda *_: (0,) * len(shape))


ANY = pl.BlockSpec(memory_space=pl.ANY)
SMEM = pl.BlockSpec(memory_space=pltpu.SMEM)


def block_of(w, base, quarter, start, n):
    q, off = divmod(start, quarter)
    if off + n <= quarter:
        return w[q, :, base + off : base + off + n, :].reshape(NF * n, LANE)
    head = quarter - off
    return jnp.concatenate(
        [w[q, :, base + off : base + quarter, :], w[q + 1, :, base : base + n - head, :]], axis=1
    ).reshape(NF * n, LANE)


def put_block(w, base, quarter, start, n, value):
    value = value.reshape(NF, n, LANE)
    q, off = divmod(start, quarter)
    if off + n <= quarter:
        w[q, :, base + off : base + off + n, :] = value
    else:
        head = quarter - off
        w[q, :, base + off : base + quarter, :] = value[:, :head]
        w[q + 1, :, base : base + n - head, :] = value[:, head:]


def columns(w, base, quarter, rows, blocks):
    return jnp.concatenate([block_of(w, base, quarter, b * rows, rows) for b in blocks], axis=1)


def put_columns(w, base, quarter, rows, blocks, value):
    for i, b in enumerate(blocks):
        put_block(w, base, quarter, b * rows, rows, value[:, i * LANE : (i + 1) * LANE])


def piece_copies(bufs, layout, idx, w, sems):
    rows = w.shape[2]
    return [
        pltpu.make_async_copy(bufs[b].at[:, pl.ds(off, rows)], w.at[idx[n]], sems.at[n])
        for n, (b, off) in enumerate(layout)
    ]


def frequency_table():
    quarter = D // 4
    frequency = 1.0 / 10000.0 ** (jnp.arange(quarter, dtype=f32) / quarter)
    angle = jnp.arange(16, dtype=f32)[:, None] * frequency
    table = jnp.concatenate([jnp.sin(angle), jnp.cos(angle)], axis=-1)
    high = table.astype(bf16)
    rest = table - high.astype(f32)
    middle = rest.astype(bf16)
    low = (rest - middle.astype(f32)).astype(bf16)
    return jnp.concatenate([high, middle, low], axis=0)


def normalised(v):
    c = v - jnp.mean(v, axis=-1, keepdims=True)
    r = lax.rsqrt(jnp.mean(c * c, axis=-1, keepdims=True) + EPS)
    return c * r, r


def norm_back(xhat, r, gain, d):
    e = gain * d
    return r * (
        e - jnp.mean(e, axis=-1, keepdims=True) - xhat * jnp.mean(e * xhat, axis=-1, keepdims=True)
    )


def start_kernel(G, cnt, table, ids, patches, upstream, start, xhat, seed, seed_sum):
    step = pl.program_id(0)

    @pl.when(step == 0)
    def _():
        seed_sum[...] = jnp.zeros_like(seed_sum)

    tab = table[...]
    place = lax.broadcasted_iota(jnp.int32, (48, SLOTS), 0) % 16
    row = lax.broadcasted_iota(jnp.int32, (SLOTS, D), 0)
    total = jnp.zeros((SLOTS, D), f32)
    for g in range(G):
        pid = ids[g]
        by_row = jnp.where(place == pid // GRID, 1.0, 0.0).astype(bf16)
        by_col = jnp.where(place == pid % GRID, 1.0, 0.0).astype(bf16)
        position = jnp.concatenate([mm(by_row, tab, TN), mm(by_col, tab, TN)], axis=1)
        v = patches[g].astype(f32) + position
        here = pl.ds(g * SLOTS, SLOTS)
        start[here, :] = v
        xhat[here, :] = normalised(v)[0]
        s = jnp.where(row < cnt[step * G + g], upstream[g].astype(f32), 0.0)
        seed[here, :] = s.astype(bf16)
        total += s
    seed_sum[...] += jnp.sum(total, axis=0, keepdims=True)


def start_call(counts, table, ids, patches, upstream):
    n = patches.shape[0]
    G = 4 if n % 4 == 0 else 1
    rows = n * SLOTS
    blk = pl.BlockSpec((G * SLOTS, D), lambda i: (i, 0))
    img = pl.BlockSpec((G, SLOTS, D), lambda i: (i, 0, 0))
    return pl.pallas_call(
        functools.partial(start_kernel, G),
        grid=(n // G,),
        in_specs=[SMEM, whole(table.shape), pl.BlockSpec((G, 1, SLOTS), lambda i: (i, 0, 0)), img, img],
        out_specs=[blk, blk, blk, whole((1, D))],
        out_shape=[
            jax.ShapeDtypeStruct((rows, D), f32),
            jax.ShapeDtypeStruct((rows, D), f32),
            jax.ShapeDtypeStruct((rows, D), bf16),
            jax.ShapeDtypeStruct((1, D), f32),
        ],
        compiler_params=params(),
        cost_estimate=pl.CostEstimate(flops=1 << 26, bytes_accessed=rows * D * 14, transcendentals=rows),
        name="start",
    )(counts, table, ids, patches, upstream)


def head_masks():
    lane = lax.broadcasted_iota(jnp.int32, (SLOTS, LANE), 1)
    return lane < HEAD_DIM


def both_heads(x, left):
    zero = jnp.zeros_like(x)
    return jnp.concatenate([jnp.where(left, x, zero), jnp.where(left, zero, x)], axis=0)


def attend_kernel(G, layout, nbuf, cnt, idx, xhat, par, *rest):
    bufs = rest[:nbuf]
    first, qkv, probs, mixed, w, sems = rest[nbuf:]
    step = pl.program_id(0)

    @pl.when(step == 0)
    def _():
        copies = piece_copies(bufs, layout, idx, w, sems)
        for c in copies:
            c.start()
        for c in copies:
            c.wait()

    x = (xhat[...] * par[0:1, :D] + par[1:2, :D]).astype(bf16)
    first[...] = x
    for part in range(3):
        cols = slice(part * D, (part + 1) * D)
        wp = columns(w, 0, QH, RB, range(part * OB, (part + 1) * OB))
        qkv[:, cols] = (mm(x, wp, NN) + par[2:3, cols]).astype(bf16)
    left = head_masks()
    key = lax.broadcasted_iota(jnp.int32, (SLOTS, SLOTS), 0)

    @pl.loop(0, G)
    def _(g):
        live = key < cnt[step * G + g]
        rows = pl.ds(pl.multiple_of(g * SLOTS, SLOTS), SLOTS)
        for p in range(HEADS // 2):
            c = p * LANE
            q = qkv[rows, c : c + LANE]
            k = qkv[rows, D + c : D + c + LANE]
            v = qkv[rows, 2 * D + c : 2 * D + c + LANE]
            s = mm(both_heads(k, left), q, NT) * HEAD_DIM**-0.5
            halves = []
            for h in range(2):
                sh = jnp.where(live, s[h * SLOTS : (h + 1) * SLOTS], NEG)
                e = jnp.exp(sh - jnp.max(sh, axis=0, keepdims=True))
                halves.append(e / jnp.sum(e, axis=0, keepdims=True))
            pt = jnp.concatenate(halves, axis=0).astype(bf16)
            probs[g, p] = pt
            mixed[rows, c : c + LANE] = mm(pt, both_heads(v, left), TN).astype(bf16)


def attend_call(counts, w, xhat, par, G=4):
    idx, bufs, layout = w
    rows = xhat.shape[0]
    n = rows // SLOTS
    G = G if n % G == 0 else 1

    def blk(width):
        return pl.BlockSpec((G * SLOTS, width), lambda i: (i, 0))

    return pl.pallas_call(
        functools.partial(attend_kernel, G, layout, len(bufs)),
        grid=(n // G,),
        in_specs=[SMEM, SMEM, blk(D), whole(par.shape)] + [ANY] * len(bufs),
        out_specs=[
            blk(D),
            blk(3 * D),
            pl.BlockSpec((G, HEADS // 2, 2 * SLOTS, SLOTS), lambda i: (i, 0, 0, 0)),
            blk(D),
        ],
        out_shape=[
            jax.ShapeDtypeStruct((rows, D), bf16),
            jax.ShapeDtypeStruct((rows, 3 * D), bf16),
            jax.ShapeDtypeStruct((n, HEADS // 2, 2 * SLOTS, SLOTS), bf16),
            jax.ShapeDtypeStruct((rows, D), bf16),
        ],
        scratch_shapes=[
            pltpu.VMEM((4, NF, QH, LANE), bf16),
            pltpu.SemaphoreType.DMA((len(layout),)),
        ],
        compiler_params=params(),
        cost_estimate=pl.CostEstimate(
            flops=2 * rows * D * 3 * D * 4, bytes_accessed=20 << 20, transcendentals=n * HEADS * 6400
        ),
        name="attend",
    )(counts, idx, xhat, par, *bufs)


def middle_kernel(layout, nbuf, idx, mixed, start, par, *rest):
    bufs = rest[:nbuf]
    middle, second, w, sems = rest[nbuf:]

    @pl.when(pl.program_id(0) == 0)
    def _():
        copies = piece_copies(bufs, layout, idx, w, sems)
        for c in copies:
            c.start()
        for c in copies:
            c.wait()

    m = start[...] + mm(mixed[...], columns(w, 0, QO, RB, range(OB)), NN) + par[3:4, :D]
    middle[...] = m
    second[...] = (normalised(m)[0] * par[4:5, :D] + par[5:6, :D]).astype(bf16)


def row_block(rows):
    return 240 if rows % 240 == 0 else SLOTS


def middle_call(w, mixed, start, par):
    idx, bufs, layout = w
    rows = mixed.shape[0]
    B = row_block(rows)
    blk = pl.BlockSpec((B, D), lambda i: (i, 0))
    return pl.pallas_call(
        functools.partial(middle_kernel, layout, len(bufs)),
        grid=(rows // B,),
        in_specs=[SMEM, blk, blk, whole(par.shape)] + [ANY] * len(bufs),
        out_specs=[blk, blk],
        out_shape=[jax.ShapeDtypeStruct((rows, D), f32), jax.ShapeDtypeStruct((rows, D), bf16)],
        scratch_shapes=[
            pltpu.VMEM((4, NF, QO, LANE), bf16),
            pltpu.SemaphoreType.DMA((len(layout),)),
        ],
        compiler_params=params(),
        cost_estimate=pl.CostEstimate(flops=2 * rows * D * D, bytes_accessed=rows * D * 12, transcendentals=rows),
        name="middle",
    )(idx, mixed, start, par, *bufs)


def gelu_and_slope(h):
    a = jnp.abs(h)
    e = jnp.exp(-0.5 * (h * h))
    t = 1.0 / (1.0 + 0.23164189 * a)
    poly = t * (
        0.127414796
        + t * (-0.142248368 + t * (0.7107068705 + t * (-0.7265760135 + t * 0.5307027145)))
    )
    tail = poly * e
    phi = jnp.where(h >= 0, 1.0 - tail, tail)
    return h * phi, phi + h * e * 0.3989422804014327


def mlp_kernel(chunk, layout, nbuf, fresh, last, widx, oidx, second, seed, res_in, dsec_in, par, *rest):
    bufs = rest[:nbuf]
    res, dsec, hsum = rest[nbuf : nbuf + 3]
    outs = rest[nbuf + 3 : nbuf + 7]
    w, ge, gr, stage, sems, osems = rest[nbuf + 7 :]
    step = pl.program_id(0)
    steps = pl.num_programs(0)

    @pl.when(step == 0)
    def _():
        copies = piece_copies(bufs, layout, widx, w, sems)
        for c in copies:
            c.start()
        ge[...] = jnp.zeros_like(ge)
        gr[...] = jnp.zeros_like(gr)
        hsum[...] = jnp.zeros_like(hsum)
        for c in copies:
            c.wait()

    x = second[...]
    s = seed[...]
    half = EB // 2
    acc = res_in[...]
    dacc = None if fresh else dsec_in[...]
    if fresh:
        acc = acc + par[7:8, :D]
    for t in range(2):
        blocks = range(t * half, (t + 1) * half)
        we = columns(w, 0, QM, RB, blocks)
        fs = slice(t * half, (t + 1) * half)
        wr = jnp.concatenate(
            [w[2 + b // 3, fs, (b % 3) * LANE : (b % 3 + 1) * LANE, :].reshape(half * LANE, LANE) for b in range(OB)],
            axis=1,
        )
        cols = slice(t * half * LANE, (t + 1) * half * LANE)
        h = mm(x, we, NN) + par[8 + chunk : 9 + chunk, cols]
        active, slope = gelu_and_slope(h)
        a = active.astype(bf16)
        dh = (mm(s, wr, NT) * slope)
        d = dh.astype(bf16)
        hsum[0:1, cols] += jnp.sum(d.astype(f32), axis=0, keepdims=True)
        acc = acc + mm(a, wr, NN)
        g = mm(d, we, NT)
        dacc = g if dacc is None else dacc + g
        ge[:, cols] += mm(x, d, TN)
        gr[cols, :] += mm(a, s, TN)
    res[...] = acc.astype(res.dtype)
    dsec[...] = dacc

    @pl.when(step == steps - 1)
    def _():
        for b in range(EB):
            stage[b // 4, :, (b % 4) * RB : (b % 4 + 1) * RB, :] = (
                ge[:, b * LANE : (b + 1) * LANE].astype(bf16).reshape(NF, RB, LANE)
            )
        for b in range(OB):
            stage[2 + b // 3, :, (b % 3) * LANE : (b % 3 + 1) * LANE, :] = (
                gr[:, b * LANE : (b + 1) * LANE].astype(bf16).reshape(NF, LANE, LANE)
            )
        copies = [
            pltpu.make_async_copy(stage.at[oidx[n]], o, osems.at[n]) for n, o in enumerate(outs)
        ]
        for c in copies:
            c.start()
        for c in copies:
            c.wait()


def mlp_call(chunk, w, oidx, second, seed, res_in, dsec_in, par):
    widx, bufs, layout = w
    rows = second.shape[0]
    B = row_block(rows)
    fresh, last = chunk == 0, chunk == CH - 1
    blk = pl.BlockSpec((B, D), lambda i: (i, 0))
    dspec = blk if not fresh else ANY
    piece = jax.ShapeDtypeStruct((NF, QM, LANE), bf16)
    return pl.pallas_call(
        functools.partial(mlp_kernel, chunk, layout, len(bufs), fresh, last),
        grid=(rows // B,),
        in_specs=[SMEM, SMEM, blk, blk, blk, dspec, whole(par.shape)] + [ANY] * len(bufs),
        out_specs=[blk, blk, whole((1, CW))] + [ANY] * 4,
        out_shape=[
            jax.ShapeDtypeStruct((rows, D), bf16 if last else f32),
            jax.ShapeDtypeStruct((rows, D), f32),
            jax.ShapeDtypeStruct((1, CW), f32),
        ]
        + [piece] * 4,
        scratch_shapes=[
            pltpu.VMEM((4, NF, QM, LANE), bf16),
            pltpu.VMEM((D, CW), f32),
            pltpu.VMEM((CW, D), f32),
            pltpu.VMEM((4, NF, QM, LANE), bf16),
            pltpu.SemaphoreType.DMA((len(layout),)),
            pltpu.SemaphoreType.DMA((4,)),
        ],
        compiler_params=params(),
        cost_estimate=pl.CostEstimate(
            flops=12 * rows * D * CW, bytes_accessed=rows * D * 20, transcendentals=rows * CW
        ),
        name="mlp",
    )(widx, oidx, second, seed, res_in, dsec_in, par, *bufs)


def branch_kernel(layout, nbuf, idx, oidx, middle, dsec, seed, mixed, par, *rest):
    bufs = rest[:nbuf]
    dmid, dmixed, sums = rest[nbuf : nbuf + 3]
    outs = rest[nbuf + 3 : nbuf + 7]
    w, acc, stage, sems, osems = rest[nbuf + 7 :]
    step = pl.program_id(0)

    @pl.when(step == 0)
    def _():
        copies = piece_copies(bufs, layout, idx, w, sems)
        for c in copies:
            c.start()
        acc[...] = jnp.zeros_like(acc)
        sums[...] = jnp.zeros_like(sums)
        for c in copies:
            c.wait()

    d = dsec[...]
    xhat, r = normalised(middle[...])
    dm = seed[...].astype(f32) + norm_back(xhat, r, par[4:5, :D], d)
    dmid[...] = dm
    db = dm.astype(bf16)
    sums[0:1, :] += jnp.sum(d * xhat, axis=0, keepdims=True)
    sums[1:2, :] += jnp.sum(d, axis=0, keepdims=True)
    sums[2:3, :] += jnp.sum(db.astype(f32), axis=0, keepdims=True)
    acc[...] += mm(mixed[...], db, TN)
    dmixed[...] = mm(db, columns(w, 0, QO, RB, range(OB)), NT).astype(bf16)

    @pl.when(step == pl.num_programs(0) - 1)
    def _():
        put_columns(stage, 0, QO, RB, range(OB), acc[...].astype(bf16))
        copies = [
            pltpu.make_async_copy(stage.at[oidx[n]], o, osems.at[n]) for n, o in enumerate(outs)
        ]
        for c in copies:
            c.start()
        for c in copies:
            c.wait()


def branch_call(w, oidx, middle, dsec, seed, mixed, par):
    idx, bufs, layout = w
    rows = mixed.shape[0]
    B = row_block(rows)
    blk = pl.BlockSpec((B, D), lambda i: (i, 0))
    return pl.pallas_call(
        functools.partial(branch_kernel, layout, len(bufs)),
        grid=(rows // B,),
        in_specs=[SMEM, SMEM, blk, blk, blk, blk, whole(par.shape)] + [ANY] * len(bufs),
        out_specs=[blk, blk, whole((8, D))] + [ANY] * 4,
        out_shape=[
            jax.ShapeDtypeStruct((rows, D), f32),
            jax.ShapeDtypeStruct((rows, D), bf16),
            jax.ShapeDtypeStruct((8, D), f32),
        ]
        + [jax.ShapeDtypeStruct((NF, QO, LANE), bf16)] * 4,
        scratch_shapes=[
            pltpu.VMEM((4, NF, QO, LANE), bf16),
            pltpu.VMEM((D, D), f32),
            pltpu.VMEM((4, NF, QO, LANE), bf16),
            pltpu.SemaphoreType.DMA((len(layout),)),
            pltpu.SemaphoreType.DMA((4,)),
        ],
        compiler_params=params(),
        cost_estimate=pl.CostEstimate(flops=4 * rows * D * D, bytes_accessed=rows * D * 20, transcendentals=rows),
        name="branch",
    )(idx, oidx, middle, dsec, seed, mixed, par, *bufs)


def attend_back_kernel(G, oidx, qkv, probs, dmixed, first, *rest):
    dproj, sums = rest[:2]
    outs = rest[2:6]
    acc, stage, osems = rest[6:]
    step = pl.program_id(0)

    @pl.when(step == 0)
    def _():
        acc[...] = jnp.zeros_like(acc)
        sums[...] = jnp.zeros_like(sums)

    left = head_masks()
    scale = HEAD_DIM**-0.5

    @pl.loop(0, G)
    def _(g):
        rows = pl.ds(pl.multiple_of(g * SLOTS, SLOTS), SLOTS)
        for p in range(HEADS // 2):
            c = p * LANE
            q = qkv[rows, c : c + LANE]
            k = qkv[rows, D + c : D + c + LANE]
            v = qkv[rows, 2 * D + c : 2 * D + c + LANE]
            do = dmixed[rows, c : c + LANE]
            pt = probs[g, p]
            dv2 = mm(pt, do, NN)
            dv = jnp.where(left, dv2[:SLOTS], dv2[SLOTS:])
            dp = mm(both_heads(v, left), do, NT)
            prob = pt.astype(f32)
            parts = []
            for h in range(2):
                ph = prob[h * SLOTS : (h + 1) * SLOTS]
                dh = dp[h * SLOTS : (h + 1) * SLOTS]
                parts.append(ph * (dh - jnp.sum(ph * dh, axis=0, keepdims=True)))
            ds = jnp.concatenate(parts, axis=0).astype(bf16)
            dk2 = mm(ds, q, NN)
            dk = jnp.where(left, dk2[:SLOTS], dk2[SLOTS:]) * scale
            dq = mm(ds, both_heads(k, left), TN) * scale
            dproj[rows, c : c + LANE] = dq.astype(bf16)
            dproj[rows, D + c : D + c + LANE] = dk.astype(bf16)
            dproj[rows, 2 * D + c : 2 * D + c + LANE] = dv.astype(bf16)

    dall = dproj[...]
    sums[0:1, :] += jnp.sum(dall.astype(f32), axis=0, keepdims=True)
    x = first[...]
    for part in range(3):
        cols = slice(part * D, (part + 1) * D)
        acc[:, cols] += mm(x, dall[:, cols], TN)

    @pl.when(step == pl.num_programs(0) - 1)
    def _():
        put_columns(stage, 0, QH, RB, range(HB), acc[...].astype(bf16))
        copies = [
            pltpu.make_async_copy(stage.at[oidx[n]], o, osems.at[n]) for n, o in enumerate(outs)
        ]
        for c in copies:
            c.start()
        for c in copies:
            c.wait()


def attend_back_call(oidx, qkv, probs, dmixed, first, G=4):
    rows = first.shape[0]
    n = rows // SLOTS
    G = G if n % G == 0 else 1
    piece = jax.ShapeDtypeStruct((NF, QH, LANE), bf16)

    def blk(width):
        return pl.BlockSpec((G * SLOTS, width), lambda i: (i, 0))

    return pl.pallas_call(
        functools.partial(attend_back_kernel, G),
        grid=(n // G,),
        in_specs=[
            SMEM,
            blk(3 * D),
            pl.BlockSpec((G, HEADS // 2, 2 * SLOTS, SLOTS), lambda i: (i, 0, 0, 0)),
            blk(D),
            blk(D),
        ],
        out_specs=[blk(3 * D), whole((8, 3 * D))] + [ANY] * 4,
        out_shape=[jax.ShapeDtypeStruct((rows, 3 * D), bf16), jax.ShapeDtypeStruct((8, 3 * D), f32)]
        + [piece] * 4,
        scratch_shapes=[
            pltpu.VMEM((D, 3 * D), f32),
            pltpu.VMEM((4, NF, QH, LANE), bf16),
            pltpu.SemaphoreType.DMA((4,)),
        ],
        compiler_params=params(),
        cost_estimate=pl.CostEstimate(
            flops=2 * rows * D * 3 * D * 5, bytes_accessed=20 << 20, transcendentals=0
        ),
        name="attend_back",
    )(oidx, qkv, probs, dmixed, first)


def input_kernel(layout, nbuf, idx, dproj, start, dmid, par, *rest):
    bufs = rest[:nbuf]
    out, sums, w, sems = rest[nbuf:]

    @pl.when(pl.program_id(0) == 0)
    def _():
        copies = piece_copies(bufs, layout, idx, w, sems)
        for c in copies:
            c.start()
        sums[...] = jnp.zeros_like(sums)
        for c in copies:
            c.wait()

    d = None
    for part in range(3):
        wp = columns(w, 0, QH, RB, range(part * OB, (part + 1) * OB))
        t = mm(dproj[:, part * D : (part + 1) * D], wp, NT)
        d = t if d is None else d + t
    xhat, r = normalised(start[...])
    sums[0:1, :] += jnp.sum(d * xhat, axis=0, keepdims=True)
    sums[1:2, :] += jnp.sum(d, axis=0, keepdims=True)
    out[...] = (dmid[...] + norm_back(xhat, r, par[0:1, :D], d)).astype(bf16)


def input_call(w, dproj, start, dmid, par):
    idx, bufs, layout = w
    rows = start.shape[0]
    B = row_block(rows)
    blk = pl.BlockSpec((B, D), lambda i: (i, 0))
    return pl.pallas_call(
        functools.partial(input_kernel, layout, len(bufs)),
        grid=(rows // B,),
        in_specs=[SMEM, pl.BlockSpec((B, 3 * D), lambda i: (i, 0)), blk, blk, whole(par.shape)]
        + [ANY] * len(bufs),
        out_specs=[blk, whole((8, D))],
        out_shape=[jax.ShapeDtypeStruct((rows, D), bf16), jax.ShapeDtypeStruct((8, D), f32)],
        scratch_shapes=[
            pltpu.VMEM((4, NF, QH, LANE), bf16),
            pltpu.SemaphoreType.DMA((len(layout),)),
        ],
        compiler_params=params(),
        cost_estimate=pl.CostEstimate(
            flops=2 * rows * D * 3 * D, bytes_accessed=rows * D * 16, transcendentals=rows
        ),
        name="input_back",
    )(idx, dproj, start, dmid, par, *bufs)


def block_major(a):
    return a.reshape(a.shape[0], -1, LANE).transpose(1, 0, 2).reshape(-1, LANE)


def from_block_major(a, rows):
    return a.reshape(-1, rows, LANE).transpose(1, 0, 2).reshape(rows, -1)


def small_rows(g1, b1, hb, ob, g2, b2, eb, rb):
    return jnp.concatenate([v.reshape(NF, -1) for v in (g1, b1, hb, ob, g2, b2, eb, rb)], axis=1)


SMALL = (("g1", RB), ("b1", RB), ("hb", 2 * RB), ("ob", RB), ("g2", RB), ("b2", RB), ("eb", FB), ("rb", RB))


def split_small(sm):
    out, at = {}, 0
    for name, width in SMALL:
        out[name] = sm[:, at : at + width]
        at += width
    return out


def par_of(sm):
    s = {k: v.astype(f32) for k, v in split_small(sm).items()}
    hb = s["hb"].reshape(2 * D)
    zero = jnp.zeros((D,), f32)
    eb = s["eb"].reshape(NF, CH, LANE).transpose(1, 0, 2).reshape(CH, CW)

    def wide(v):
        return jnp.pad(v, (0, FF - v.shape[0]))

    rows = [
        s["g1"].reshape(D),
        s["b1"].reshape(D),
        jnp.concatenate([hb[:D], zero, hb[D:]]),
        s["ob"].reshape(D),
        s["g2"].reshape(D),
        s["b2"].reshape(D),
        zero,
        s["rb"].reshape(D),
        eb[0],
        eb[1],
        eb[2],
    ]
    rows += [zero] * 5
    return jnp.stack([wide(r) for r in rows])


def small_grads(seed_sum, hsums, bsums, hbsum, isums):
    eb = jnp.stack([h[0] for h in hsums]).reshape(CH, NF, LANE).transpose(1, 0, 2).reshape(FF)
    hb = jnp.concatenate([hbsum[0, :D], hbsum[0, 2 * D :]])
    return small_rows(isums[0], isums[1], hb, bsums[2], bsums[0], bsums[1], eb, seed_sum[0])


def chain(counts, ids, patches, upstream, table, hooks):
    n = patches.shape[0]
    start, xhat, seed, seed_sum = start_call(counts, table, ids.reshape(n, 1, SLOTS), patches, upstream)
    hw, par = hooks.heads()
    first, qkv, probs, mixed = attend_call(counts, hw, xhat, par)
    ow = hooks.out()
    middle, second = middle_call(ow, mixed, start, par)
    res, dsec = middle, jnp.zeros((8, LANE), f32)
    hsums = []
    for j in range(CH):
        res, dsec, hs, *pieces = mlp_call(j, hooks.mlp(j), hooks.order, second, seed, res, dsec, par)
        hsums.append(hs)
        hooks.grads("m%d" % j, pieces)
    dmid, dmixed, bsums, *pieces = branch_call(ow, hooks.order, middle, dsec, seed, mixed, par)
    hooks.grads("o", pieces)
    dproj, hbsum, *pieces = attend_back_call(hooks.order, qkv, probs, dmixed, first)
    hooks.grads("h", pieces)
    pgrad, isums = input_call(hw, dproj, start, dmid, par)
    smalls = small_grads(seed_sum, hsums, bsums, hbsum, isums)
    return res.reshape(n, SLOTS, D), pgrad.reshape(n, SLOTS, D), hooks.finish(smalls)


FOUR = tuple((b, 0) for b in range(4))


class Plain:
    def __init__(self, args):
        self.full = {k: lax.all_gather(v, "fsdp", axis=0, tiled=True) for k, v in args.items()}
        self.order = jnp.arange(4, dtype=jnp.int32)
        self.got = {}

    def pieces(self, a, quarter):
        return self.order, [a[:, q * quarter : (q + 1) * quarter] for q in range(4)], FOUR

    def heads(self):
        f = self.full
        sm = small_rows(*(f[k] for k, _ in SMALL))
        w = jax.vmap(block_major)(f["hw"].reshape(NF, RB, 3 * D))
        return self.pieces(w, QH), par_of(sm)

    def out(self):
        return self.pieces(jax.vmap(block_major)(self.full["ow"].reshape(NF, RB, D)), QO)

    def mlp(self, j):
        e = self.full["ew"].reshape(NF, RB, NF, CH, LANE)[:, :, :, j].transpose(0, 2, 1, 3)
        r = self.full["rw"].reshape(NF, CH, LANE, OB, LANE)[:, j].transpose(0, 2, 1, 3)
        w = jnp.concatenate([e.reshape(NF, -1, LANE), r.reshape(NF, -1, LANE)], axis=1)
        return self.pieces(w, QM)

    def grads(self, name, pieces):
        self.got[name] = jnp.concatenate(pieces, axis=1)

    def finish(self, smalls):
        g = self.got
        hw = jax.vmap(lambda a: from_block_major(a, RB))(g["h"]).reshape(D, 3 * D)
        ow = jax.vmap(lambda a: from_block_major(a, RB))(g["o"]).reshape(D, D)
        e = jnp.stack([g["m%d" % j][:, : EB * RB].reshape(NF, NF, RB, LANE) for j in range(CH)])
        ew = e.transpose(1, 3, 2, 0, 4).reshape(D, FF)
        r = jnp.stack([g["m%d" % j][:, EB * RB :].reshape(NF, OB, LANE, LANE) for j in range(CH)])
        rw = r.transpose(1, 0, 3, 2, 4).reshape(FF, D)
        s = {k: v.reshape(-1) for k, v in split_small(smalls).items()}
        s.update(hw=hw, ow=ow, ew=ew, rw=rw)

        def total(v):
            part = lax.psum_scatter(v.astype(bf16), "fsdp", scatter_dimension=0, tiled=True)
            return lax.psum(part, "rep").astype(f32)

        return {k: total(v) for k, v in s.items()}


CORE = ((0, 1), (1, 0), (2, 3), (3, 2))
ACROSS = ((0, 2), (2, 0), (1, 3), (3, 1))


def to_core(a):
    return lax.ppermute(a, "rep", CORE)


def to_across(a):
    return lax.ppermute(a, "rep", ACROSS)


def gathered(a):
    return lax.all_gather(a[None], "fsdp", axis=0, tiled=True)


class Fast:
    def __init__(self, args):
        rep = lax.axis_index("rep")
        y, c = rep // 2, rep % 2
        self.y, self.c = y, c
        q = 2 * c + y
        self.order = jnp.stack([q, q ^ 1, q ^ 2, q ^ 3]).astype(jnp.int32)
        self.got = {}
        sm = jnp.concatenate([args[k] for k, _ in SMALL]).reshape(9, LANE)
        hw = lax.dynamic_slice_in_dim(block_major(args["hw"]), c * 2 * QH, 2 * QH, 0)
        hw = jnp.concatenate([hw, sm, jnp.zeros((SM - 9, LANE), bf16)], axis=0)
        ow = lax.dynamic_slice_in_dim(block_major(args["ow"]), q * QO, QO, 0)
        e = args["ew"].reshape(RB, NF, CH, LANE).transpose(2, 1, 0, 3).reshape(CH, -1, LANE)
        r = args["rw"].reshape(CH, LANE, OB, LANE).transpose(0, 2, 1, 3).reshape(CH, -1, LANE)
        m = jnp.concatenate([e, r], axis=1)
        m = lax.dynamic_slice_in_dim(m, q * QM, QM, 1)
        self.h = gathered(hw)
        self.h2 = to_core(self.h)
        self.a = self.spread(gathered(jnp.concatenate([ow, m[0]], axis=0)))
        self.b = self.spread(gathered(jnp.concatenate([m[1], m[2]], axis=0)))

    def spread(self, a):
        b = to_across(a)
        return [a, b, to_core(a), to_core(b)]

    def heads(self):
        c = self.c
        idx = jnp.stack([2 * c, 2 * c + 1, 2 - 2 * c, 3 - 2 * c]).astype(jnp.int32)
        par = par_of(self.h[:, 2 * QH : 2 * QH + 9].reshape(NF, 9 * LANE))
        return (idx, [self.h, self.h2], ((0, 0), (0, QH), (1, 0), (1, QH))), par

    def out(self):
        return self.order, self.a, FOUR

    def mlp(self, j):
        if j == 0:
            return self.order, self.a, tuple((b, QO) for b in range(4))
        return self.order, self.b, tuple((b, (j - 1) * QM) for b in range(4))

    def grads(self, name, pieces):
        self.got[name] = pieces

    def to_quarter(self, pieces):
        a0 = pieces[0] + to_core(pieces[2])
        a1 = pieces[1] + to_core(pieces[3])
        return a0 + to_across(a1)

    def reduced(self, b):
        return lax.psum_scatter(b, "fsdp", scatter_dimension=0, tiled=True)[0]

    def whole_shard(self, own):
        across = to_across(own)
        half = jnp.where(self.y == 0, jnp.concatenate([own, across], 1), jnp.concatenate([across, own], 1))
        other = to_core(half)
        return jnp.where(self.c == 0, jnp.concatenate([half, other], 1), jnp.concatenate([other, half], 1))

    def finish(self, smalls):
        m = [self.reduced(self.to_quarter(self.got["m%d" % j])) for j in range(CH)]
        m = self.whole_shard(jnp.stack(m))
        e = m[:, : EB * RB].reshape(CH, NF, RB, LANE)
        r = m[:, EB * RB :].reshape(CH, OB, LANE, LANE)
        out = {
            "ew": e.transpose(2, 1, 0, 3).reshape(RB, FF).astype(f32),
            "rw": r.transpose(0, 2, 1, 3).reshape(FB, D).astype(f32),
        }
        s = smalls.astype(bf16).reshape(NF, 9, LANE)
        s = s + to_core(s)
        s = s + to_across(s)
        h = self.to_quarter(self.got["h"])
        o = self.to_quarter(self.got["o"])
        h = self.reduced(jnp.concatenate([h, o, s], axis=1))
        sm = split_small(h[QH + QO :].reshape(1, 9 * LANE).astype(f32))
        out.update({k: v[0] for k, v in sm.items()})
        hw = self.whole_shard(h[None, :QH])[0]
        ow = self.whole_shard(h[None, QH : QH + QO])[0]
        out["hw"] = from_block_major(hw, RB).astype(f32)
        out["ow"] = from_block_major(ow, RB).astype(f32)
        return out


NAMES = ("g1", "b1", "hw", "hb", "ow", "ob", "g2", "b2", "ew", "eb", "rw", "rb")


def body(fast, patches, visible_count, patch_index, *rest):
    args = dict(zip(NAMES, rest[:12]))
    upstream = rest[12]
    hooks = (Fast if fast else Plain)(args)
    out, pgrad, g = chain(visible_count, patch_index, patches, upstream, frequency_table(), hooks)
    return (out, pgrad) + tuple(g[k] for k in NAMES)


def solution(mesh):
    rows = P(("rep", "fsdp"), None, None)
    mat, vec = P("fsdp", None), P("fsdp")
    weights = tuple(mat if k[1] == "w" else vec for k in NAMES)
    fast = mesh.shape["fsdp"] == NF and mesh.shape["rep"] == 4
    return jax.shard_map(
        functools.partial(body, fast),
        mesh=mesh,
        in_specs=(rows, P(("rep", "fsdp")), P(("rep", "fsdp"), None)) + weights + (rows,),
        out_specs=(rows, rows) + weights,
        check_vma=False,
    )
```

time: 942 us -> 499 us (0.53)
  waiting for transfers between devices: 501 us -> 266 us
  Pallas kernels: 0 us -> 140 us
  matrix products: 128 us -> 0 us
  blocking collectives: 108 us -> 0 us
  local copies, waits for them, and re-layouts: 112 us -> 36.2 us
  other arithmetic: 62.7 us -> 23.3 us
  starting transfers between devices: 0.61 us -> 16.4 us
    reduce_scatter x4, waiting for transfers between devices: 399 us -> 116 us  [reduced(): return lax.psum_scatter(b, 'fsdp', scatter_dimension=0, tiled=True)[0]]
    pallas_call x0 -> x9, Pallas kernels: none -> 140 us  [the longest x3 57.2 us: mlp_call(): pl.pallas_call(functools.partial(mlp_kernel, chunk, layout, len(bufs), fr...]
    dot_general x18 -> x0, matrix products: 128 us -> none  [the longest x1 36.1 us: body(): d_active = jnp.dot(seed, reduce_back.T, preferred_element_type=jnp.float32)]
    unnamed x2 -> x0, blocking collectives: 75.7 us -> none
    convert_element_type x31 -> x3, other arithmetic: 40.9 us -> 0.23 us  [the longest x1 0.08 us: frequency_table(): middle = rest.astype(bf16)]
    convert_element_type x3 -> x6, local copies, waits for them, and re-layouts: 36 us -> 3.28 us  [the longest x2 1.99 us: finish(): e.transpose(2, 1, 0, 3).reshape(RB, FF).astype(f32)]
    unnamed x145 -> x63, local copies, waits for them, and re-layouts: 37.7 us -> 7.48 us
    ppermute x0 -> x30, waiting for transfers between devices: none -> 27.7 us  [the longest x11 21.5 us: to_across(): return lax.ppermute(a, 'rep', ACROSS)]
  transfers between devices with their start and end apart: 9 -> 37, of which waited for: 5 -> 14; matrix products, arithmetic and copies ran while one was open for 25% -> 10% of each run, Pallas kernels for 0% -> 28%
where the time goes in v1:
time: 499 us; the launch traced here: 497 us
  waiting for transfers between devices  266 us (53%)
  Pallas kernels  140 us (28%)
  local copies, waits for them, and re-layouts  36.2 us (7%)
  other arithmetic  23.3 us (5%)
  starting transfers between devices  16.4 us (3%)
  between operations  15 us (3%)
    all_gather x3, waiting for transfers between devices, gathered(): return lax.all_gather(a[None], 'fsdp', axis=0, tiled=True)  122 us
    reduce_scatter x4, waiting for transfers between devices, reduced(): return lax.psum_scatter(b, 'fsdp', scatter_dimension=0, tiled=True)[0]  116 us
    pallas_call x3, Pallas kernels, mlp_call(): pl.pallas_call(functools.partial(mlp_kernel, chunk, layout, len(bufs), fr...  57.2 us
    pallas_call x1, Pallas kernels, attend_back_call(): pl.pallas_call(functools.partial(attend_back_kernel, G), grid=(n // G,),...  30.8 us
    ppermute x11, waiting for transfers between devices, to_across(): return lax.ppermute(a, 'rep', ACROSS)  21.5 us
    pallas_call x1, Pallas kernels, attend_call(): pl.pallas_call(functools.partial(attend_kernel, G, layout, len(bufs)), gr...  16.2 us
    ppermute x11, starting transfers between devices, to_across(): return lax.ppermute(a, 'rep', ACROSS)  12.6 us
    pallas_call x1, Pallas kernels, branch_call(): pl.pallas_call(functools.partial(branch_kernel, layout, len(bufs)), grid=...  11.8 us
  transfers between devices with their start and end apart: 37, of which 14 were waited for; matrix products, arithmetic and copies ran while one was open for 10% of the time, Pallas kernels for 28%

profile of v1, /device:TPU:0, one launch (start us, length us, event | category | flops | bytes accessed | tf_op | source)
XLA Modules:
  0.0 497.2 jit_solution(14383468372035258940)
XLA Ops:
  7.3 1.1 reshape.354
  8.4 1.9 reshape.356
  14.9 40.8 %all-gather.9.cloned.1.call-done = bf16[4224,128]{1,0:T(8,128)(2,1)} async-done(((bf16[528,128]{1,0:T(8,128)(2,1)}), bf16[4224,128]{1,0:T(8,128)(2,1)}) %all-gather.9.cloned.1.call-update) | async-done | bytes 1081360 | tf_op jit(solution)/shard_map/all_gather | solution.py:766
  55.7 1.5 collective-permute-start.1
  58.7 5.9 %start.1 = (f32[960,768]{1,0:T(8,128)}, f32[960,768]{1,0:T(8,128)}, bf16[960,768]{1,0:T(8,128)(2,1)}, f32[1,768]{1,0:T(1,128)}) custom-call(s32[12]{0:T(128)} %cnt.3, bf16[48,384]{1,0:T(8,128)(2,1)} %pad_maximum_fusion.3.table, s32[12,1,80]{2,1,0:T(1,128)} %reshape.342.ids, bf16[12,80,768]{2,1,0:T(8,128)(2,1)} %patches.1, bf16[12,80,768]{2,1,0:T(8,128)(2,1)} %upstream.1), custom_call_target="tpu_custom_call" | custom-call | flops 67108864 | bytes 10321920 | tf_op jit(solution)/shard_map/start/pallas_call | solution.py:152
  65.7 35.8 %all-gather.11.cloned.1.call-done = bf16[6144,128]{1,0:T(8,128)(2,1)} async-done(((bf16[768,128]{1,0:T(8,128)(2,1)}), bf16[6144,128]{1,0:T(8,128)(2,1)}) %all-gather.11.cloned.1.call-update) | async-done | bytes 1572880 | tf_op jit(solution)/shard_map/all_gather | solution.py:766
  101.6 1.5 collective-permute-start.4
  103.3 45.8 %all-gather.7.cloned.1.call-done = bf16[7040,128]{1,0:T(8,128)(2,1)} async-done(((bf16[880,128]{1,0:T(8,128)(2,1)}), bf16[7040,128]{1,0:T(8,128)(2,1)}) %all-gather.7.cloned.1.call-update) | async-done | bytes 1802256 | tf_op jit(solution)/shard_map/all_gather | solution.py:766
  150.9 1.6 stack.123.par
  154.0 16.2 %attend.1 = (bf16[960,768]{1,0:T(8,128)(2,1)}, bf16[960,2304]{1,0:T(8,128)(2,1)}, bf16[12,6,160,80]{3,2,1,0:T(8,128)(2,1)}, bf16[960,768]{1,0:T(8,128)(2,1)}) custom-call(s32[12]{0:T(128)} %cnt.3, s32[4]{0:T(128)} %pad_add_fusion.1.idx, f32[960,768]{1,0:T(8,128)} %get-tuple-element.60.xhat, f32[16,3072]{1,0:T(8,128)} %stack.123.par, ...), custom_call_target="tpu_custom_call" | custom-call | flops 13589544960 | bytes 20971520 | tf_op jit(solution)/shard_map/attend/pallas_call | solution.py:230
  171.2 7.1 %middle.1 = (f32[960,768]{1,0:T(8,128)}, bf16[960,768]{1,0:T(8,128)(2,1)}) custom-call(s32[4]{0:T(128)} %pad_add_fusion.idx.widx.oidx, bf16[960,768]{1,0:T(8,128)(2,1)} %get-tuple-element.61.mixed, f32[960,768]{1,0:T(8,128)} %get-tuple-element.62.start, f32[16,3072]{1,0:T(8,128)} %stack.123.par, bf16[8,528,128]{2,1,0:T(8,128)(2,1)} %bitcast.117, ...), custom_call_target="tpu_custom_call" | custom-call | flops 1132462080 | bytes 8847360 | tf_op jit(solution)/shard_map/middle/pallas_call | solution.py:284
  178.8 18.8 %mlp.3 = (f32[960,768]{1,0:T(8,128)}, f32[960,768]{1,0:T(8,128)}, f32[1,1024]{1,0:T(1,128)}, bf16[8,384,128]{2,1,0:T(8,128)(2,1)}, bf16[8,384,128]{2,1,0:T(8,128...) custom-call(s32[4]{0:T(128)} %pad_add_fusion.idx.widx.oidx, s32[4]{0:T(128)} %pad_add_fusion.idx.widx.oidx, ...), custom_call_target="tpu_custom_call" | custom-call | flops 9059696640 | bytes 14745600 | tf_op jit(solution)/shard_map/mlp/pallas_call | solution.py:389
  198.3 2.0 collective-permute-done.20
  200.3 1.3 add.116
  201.6 1.5 collective-permute-start.21
  203.1 19.3 %mlp.4 = (f32[960,768]{1,0:T(8,128)}, f32[960,768]{1,0:T(8,128)}, f32[1,1024]{1,0:T(1,128)}, bf16[8,384,128]{2,1,0:T(8,128)(2,1)}, bf16[8,384,128]{2,1,0:T(8,128...) custom-call(s32[4]{0:T(128)} %pad_add_fusion.idx.widx.oidx, s32[4]{0:T(128)} %pad_add_fusion.idx.widx.oidx, ...), custom_call_target="tpu_custom_call" | custom-call | flops 9059696640 | bytes 14745600 | tf_op jit(solution)/shard_map/mlp/pallas_call | solution.py:389
  223.7 19.0 %mlp.5 = (bf16[960,768]{1,0:T(8,128)(2,1)}, f32[960,768]{1,0:T(8,128)}, f32[1,1024]{1,0:T(1,128)}, bf16[8,384,128]{2,1,0:T(8,128)(2,1)}, bf16[8,384,128]{2,1,0:T...) custom-call(s32[4]{0:T(128)} %pad_add_fusion.idx.widx.oidx, s32[4]{0:T(128)} %pad_add_fusion.idx.widx.oidx, ...), custom_call_target="tpu_custom_call" | custom-call | flops 9059696640 | bytes 14745600 | tf_op jit(solution)/shard_map/mlp/pallas_call | solution.py:389
  245.2 11.8 %branch.1 = (f32[960,768]{1,0:T(8,128)}, bf16[960,768]{1,0:T(8,128)(2,1)}, f32[8,768]{1,0:T(8,128)}, bf16[8,144,128]{2,1,0:T(8,128)(2,1)}, bf16[8,144,128]{2,1,0...) custom-call(s32[4]{0:T(128)} %pad_add_fusion.idx.widx.oidx, s32[4]{0:T(128)} %pad_add_fusion.idx.widx.oidx, ...), custom_call_target="tpu_custom_call" | custom-call | flops 2264924160 | bytes 14745600 | tf_op jit(solution)/shard_map/branch/pallas_call | solution.py:461
  257.1 2.3 add.122
  259.4 1.5 collective-permute-start.27
  260.8 4.2 collective-permute-done.24
  266.2 30.8 %attend_back.1 = (bf16[960,2304]{1,0:T(8,128)(2,1)}, f32[8,2304]{1,0:T(8,128)}, bf16[8,432,128]{2,1,0:T(8,128)(2,1)}, bf16[8,432,128]{2,1,0:T(8,128)(2,1)}, bf16...) custom-call(s32[4]{0:T(128)} %pad_add_fusion.idx.widx.oidx, bf16[960,2304]{1,0:T(8,128)(2,1)} %get-tuple-element.71.qkv, ...), custom_call_target="tpu_custom_call" | custom-call | flops 16986931200 | bytes 20971520 | tf_op jit(solution)/shard_map/attend_back/pallas_call | solution.py:554
  300.4 2.2 add_add_fusion.1
  302.7 11.0 %input_back.1 = (bf16[960,768]{1,0:T(8,128)(2,1)}, f32[8,768]{1,0:T(8,128)}) custom-call(s32[4]{0:T(128)} %pad_add_fusion.1.idx, bf16[960,2304]{1,0:T(8,128)(2,1)} %get-tuple-element.76.dproj, f32[960,768]{1,0:T(8,128)} %get-tuple-element.62.start, f32[960,768]{1,0:T(8,128)} %get-tuple-element.77.dmid, f32[16,3072]{1,0:T(8,128)} %stack.123.par, ...), custom_call_target="tpu_custom_call" | custom-call | flops 3397386240 | bytes 11796480 | tf_op jit(solution)/shard_map/input_back/pallas_call | solution.py:609
  315.9 1.4 concatenate.136
  317.3 1.4 slice_reduce_fusion.5
  319.3 1.8 add.111
  321.1 1.5 collective-permute-start.12
  324.0 1.3 reshape_squeeze.27
  325.3 1.3 reshape_squeeze.26
  326.6 1.3 reshape_squeeze.30
  328.0 1.4 reshape_squeeze.29
  329.3 1.3 reshape_squeeze.28
  330.6 1.4 concatenate.139
  332.8 1.2 collective-permute-done.13
  335.2 7.5 %collective-permute-done.14 = bf16[8,9,128]{2,1,0:T(8,128)(2,1)S(1)} collective-permute-done((bf16[8,9,128]{2,1,0:T(8,128)(2,1)S(1)}, bf16[8,9,128]{2,1,0:T(8,128)(2,1)S(1)}, u32[]{:S(2)}, u32[]{:S(2)}) %collective-permute-start.14) | collective-permute-done | bytes 18464 | tf_op jit(solution)/shard_map/ppermute | solution.py:762
  342.8 1.2 add_add_fusion.4
  344.2 1.2 pad_maximum_fusion
  346.3 3.3 reduce-scatter.9.cloned.1.call-done
  350.5 63.7 %reduce-scatter.11.cloned.1.call-done = bf16[1,384,128]{2,1,0:T(8,128)(2,1)} async-done(((bf16[8,384,128]{2,1,0:T(8,128)(2,1)}), bf16[1,384,128]{2,1,0:T(8,128)(2,1)}) %reduce-scatter.11.cloned.1.call-update) | async-done | bytes 98320 | tf_op jit(solution)/shard_map/reduce_scatter | solution.py:817
  415.1 1.5 collective-permute-start.28
  416.5 5.6 %collective-permute-done.28 = bf16[3,384,128]{2,1,0:T(8,128)(2,1)S(1)} collective-permute-done((bf16[3,384,128]{2,1,0:T(8,128)(2,1)S(1)}, bf16[3,384,128]{2,1,0:T(8,128)(2,1)S(1)}, u32[]{:S(2)}, u32[]{:S(2)}) %collective-permute-start.28) | collective-permute-done | bytes 294944 | tf_op jit(solution)/shard_map/ppermute | solution.py:762
  422.4 2.0 collective-permute-done.29
  425.3 1.5 reshape.372
  427.2 1.3 copy.69
  428.4 49.0 %reduce-scatter.5.cloned.1.call-done = bf16[1,585,128]{2,1,0:T(8,128)(2,1)} async-done(((bf16[8,585,128]{2,1,0:T(8,128)(2,1)}), bf16[1,585,128]{2,1,0:T(8,128)(2,1)}) %reduce-scatter.5.cloned.1.call-update) | async-done | bytes 149776 | tf_op jit(solution)/shard_map/reduce_scatter | solution.py:817
  478.9 1.5 collective-permute-start.17
  483.2 4.1 collective-permute-done.15
  (211 shorter events, 38.6 us)
Async XLA Ops:
  7.2 48.5 %all-gather.9.cloned.1.call-start = ((), (), s32[]{:S(2)}) async-start(), calls=%async_computation.9 | async-start | bytes 1216512 | tf_op jit(solution)/shard_map/all_gather | solution.py:766
  12.6 89.0 %all-gather.11.cloned.1.call-start = ((), (), s32[]{:S(2)}) async-start(), calls=%async_computation.10 | async-start | bytes 1769472 | tf_op jit(solution)/shard_map/all_gather | solution.py:766
  13.3 135.8 %all-gather.7.cloned.1.call-start = ((), (), s32[]{:S(2)}) async-start(), calls=%async_computation.8 | async-start | bytes 2027520 | tf_op jit(solution)/shard_map/all_gather | solution.py:766
  13.4 43.8 %copy-start.14 = (s32[12,80]{1,0:T(8,128)S(1)}, s32[12,80]{1,0:T(8,128)}, u32[]{:S(2)}) copy-start(s32[12,80]{1,0:T(8,128)} %param.18) | copy-start | bytes 11524
  14.9 330.5 %reduce-scatter.7.cloned.1.call-start = ((), (), s32[]{:S(2)}) async-start(), calls=%async_computation.5 | async-start | bytes 884736 | tf_op jit(solution)/shard_map/reduce_scatter | solution.py:817
  55.7 47.3 %collective-permute-start.1 = (bf16[8,528,128]{2,1,0:T(8,128)(2,1)}, bf16[8,528,128]{2,1,0:T(8,128)(2,1)S(1)}, u32[]{:S(2)}, u32[]{:S(2)}) collective-permute-start(bf16[8,528,128]{2,1,0:T(8,128)(2,1)} %bitcast.116), channel_id=1, source_target_pairs={{0,16},{16,0},{8,24},{24,8},{1,17},{17,1},{9,25},{25,9},{2,18},{18... | collective-permute-start | bytes 3244040 | tf_op jit(solution)/shard_map/ppermute | solution.py:762
  65.7 104.4 %collective-permute-start.2 = (bf16[8,528,128]{2,1,0:T(8,128)(2,1)S(1)}, bf16[8,528,128]{2,1,0:T(8,128)(2,1)S(1)}, u32[]{:S(2)}, u32[]{:S(2)}) collective-permute-start(bf16[8,528,128]{2,1,0:T(8,128)(2,1)S(1)} %bitcast.120), channel_id=1, source_target_pairs={{0,8},{8,0},{16,24},{24,16},{1,9},{9,1},{17,25},{25,17},{2,10},{10... | collective-permute-start | bytes 3244040 | tf_op jit(solution)/shard_map/ppermute | solution.py:758
  101.6 101.6 %collective-permute-start.5 = (bf16[8,768,128]{2,1,0:T(8,128)(2,1)}, bf16[8,768,128]{2,1,0:T(8,128)(2,1)}, u32[]{:S(2)}, u32[]{:S(2)}) collective-permute-start(bf16[8,768,128]{2,1,0:T(8,128)(2,1)} %bitcast.168), channel_id=1, source_target_pairs={{0,8},{8,0},{16,24},{24,16},{1,9},{9,1},{17,25},{25,17},{2,10},{10... | collective-permute-start | bytes 4718600 | tf_op jit(solution)/shard_map/ppermute | solution.py:758
  101.6 50.9 %collective-permute-start.4 = (bf16[8,768,128]{2,1,0:T(8,128)(2,1)}, bf16[8,768,128]{2,1,0:T(8,128)(2,1)}, u32[]{:S(2)}, u32[]{:S(2)}) collective-permute-start(bf16[8,768,128]{2,1,0:T(8,128)(2,1)} %bitcast.169), channel_id=1, source_target_pairs={{0,16},{16,0},{8,24},{24,8},{1,17},{17,1},{9,25},{25,9},{2,18},{18... | collective-permute-start | bytes 4718600 | tf_op jit(solution)/shard_map/ppermute | solution.py:762
  103.1 67.1 %copy-start.1 = (bf16[8,528,128]{2,1,0:T(8,128)(2,1)}, bf16[8,528,128]{2,1,0:T(8,128)(2,1)S(1)}, u32[]{:S(2)}) copy-start(bf16[8,528,128]{2,1,0:T(8,128)(2,1)S(1)} %collective-permute-done.1.rest_1_) | copy-start | bytes 3244036
  103.1 67.2 %collective-permute-start.3 = (bf16[8,528,128]{2,1,0:T(8,128)(2,1)S(1)}, bf16[8,528,128]{2,1,0:T(8,128)(2,1)}, u32[]{:S(2)}, u32[]{:S(2)}) collective-permute-start(bf16[8,528,128]{2,1,0:T(8,128)(2,1)S(1)} %collective-permute-done.1.rest_1_), channel_id=1, source_target_pairs={{0,8},{8,0},{16,24},{24,16},{1,9},{9,1},{17,25},{25,17},{2,10},{10... | collective-permute-start | bytes 3244040 | tf_op jit(solution)/shard_map/ppermute | solution.py:758
  149.9 4.1 collective-permute-start
  152.5 50.6 %collective-permute-start.6 = (bf16[8,768,128]{2,1,0:T(8,128)(2,1)}, bf16[8,768,128]{2,1,0:T(8,128)(2,1)}, u32[]{:S(2)}, u32[]{:S(2)}) collective-permute-start(bf16[8,768,128]{2,1,0:T(8,128)(2,1)} %collective-permute-done.4.rest_1_), channel_id=1, source_target_pairs={{0,8},{8,0},{16,24},{24,16},{1,9},{9,1},{17,25},{25,17},{2,10},{10... | collective-permute-start | bytes 4718600 | tf_op jit(solution)/shard_map/ppermute | solution.py:758
  197.7 2.6 collective-permute-start.20
  197.9 24.7 %collective-permute-start.19 = (bf16[8,384,128]{2,1,0:T(8,128)(2,1)}, bf16[8,384,128]{2,1,0:T(8,128)(2,1)S(1)}, u32[]{:S(2)}, u32[]{:S(2)}) collective-permute-start(bf16[8,384,128]{2,1,0:T(8,128)(2,1)} %get-tuple-element.95), channel_id=1, source_target_pairs={{0,8},{8,0},{16,24},{24,16},{1,9},{9,1},{17,25},{25,17},{2,10},{10... | collective-permute-start | bytes 2359304 | tf_op jit(solution)/shard_map/ppermute | solution.py:758
  201.6 21.0 %collective-permute-start.21 = (bf16[8,384,128]{2,1,0:T(8,128)(2,1)S(1)}, bf16[8,384,128]{2,1,0:T(8,128)(2,1)S(1)}, u32[]{:S(2)}, u32[]{:S(2)}) collective-permute-start(bf16[8,384,128]{2,1,0:T(8,128)(2,1)S(1)} %add.116), channel_id=1, source_target_pairs={{0,16},{16,0},{8,24},{24,8},{1,17},{17,1},{9,25},{25,9},{2,18},{18... | collective-permute-start | bytes 2359304 | tf_op jit(solution)/shard_map/ppermute | solution.py:762
  203.1 19.4 %copy-start.9 = (bf16[8,384,128]{2,1,0:T(8,128)(2,1)S(1)}, bf16[8,384,128]{2,1,0:T(8,128)(2,1)}, u32[]{:S(2)}) copy-start(bf16[8,384,128]{2,1,0:T(8,128)(2,1)} %get-tuple-element.94) | copy-start | bytes 2359300
  222.5 20.9 %collective-permute-start.23 = (bf16[8,384,128]{2,1,0:T(8,128)(2,1)}, bf16[8,384,128]{2,1,0:T(8,128)(2,1)S(1)}, u32[]{:S(2)}, u32[]{:S(2)}) collective-permute-start(bf16[8,384,128]{2,1,0:T(8,128)(2,1)} %get-tuple-element.101), channel_id=1, source_target_pairs={{0,8},{8,0},{16,24},{24,16},{1,9},{9,1},{17,25},{25,17},{2,10},{10... | collective-permute-start | bytes 2359304 | tf_op jit(solution)/shard_map/ppermute | solution.py:758
  223.7 125.9 %reduce-scatter.9.cloned.1.call-start = ((), (), s32[]{:S(2)}) async-start(), calls=%async_computation.6 | async-start | bytes 884736 | tf_op jit(solution)/shard_map/reduce_scatter | solution.py:817
  223.7 19.7 %copy-start.7 = (bf16[8,384,128]{2,1,0:T(8,128)(2,1)S(1)}, bf16[8,384,128]{2,1,0:T(8,128)(2,1)}, u32[]{:S(2)}) copy-start(bf16[8,384,128]{2,1,0:T(8,128)(2,1)} %get-tuple-element.100) | copy-start | bytes 2359300
  242.8 14.3 %collective-permute-start.26 = (bf16[8,384,128]{2,1,0:T(8,128)(2,1)}, bf16[8,384,128]{2,1,0:T(8,128)(2,1)}, u32[]{:S(2)}, u32[]{:S(2)}) collective-permute-start(bf16[8,384,128]{2,1,0:T(8,128)(2,1)} %get-tuple-element.105), channel_id=1, source_target_pairs={{0,8},{8,0},{16,24},{24,16},{1,9},{9,1},{17,25},{25,17},{2,10},{10... | collective-permute-start | bytes 2359304 | tf_op jit(solution)/shard_map/ppermute | solution.py:758
  243.3 17.5 %collective-permute-start.22 = (bf16[8,384,128]{2,1,0:T(8,128)(2,1)}, bf16[8,384,128]{2,1,0:T(8,128)(2,1)S(1)}, u32[]{:S(2)}, u32[]{:S(2)}) collective-permute-start(bf16[8,384,128]{2,1,0:T(8,128)(2,1)} %get-tuple-element.99), channel_id=1, source_target_pairs={{0,8},{8,0},{16,24},{24,16},{1,9},{9,1},{17,25},{25,17},{2,10},{10... | collective-permute-start | bytes 2359304 | tf_op jit(solution)/shard_map/ppermute | solution.py:758
  244.5 20.6 %collective-permute-start.24 = (bf16[8,384,128]{2,1,0:T(8,128)(2,1)}, bf16[8,384,128]{2,1,0:T(8,128)(2,1)S(1)}, u32[]{:S(2)}, u32[]{:S(2)}) collective-permute-start(bf16[8,384,128]{2,1,0:T(8,128)(2,1)} %add.119), channel_id=1, source_target_pairs={{0,16},{16,0},{8,24},{24,8},{1,17},{17,1},{9,25},{25,9},{2,18},{18... | collective-permute-start | bytes 2359304 | tf_op jit(solution)/shard_map/ppermute | solution.py:762
  245.1 54.9 %collective-permute-start.25 = (bf16[8,384,128]{2,1,0:T(8,128)(2,1)}, bf16[8,384,128]{2,1,0:T(8,128)(2,1)S(1)}, u32[]{:S(2)}, u32[]{:S(2)}) collective-permute-start(bf16[8,384,128]{2,1,0:T(8,128)(2,1)} %get-tuple-element.103), channel_id=1, source_target_pairs={{0,8},{8,0},{16,24},{24,16},{1,9},{9,1},{17,25},{25,17},{2,10},{10... | collective-permute-start | bytes 2359304 | tf_op jit(solution)/shard_map/ppermute | solution.py:758
  245.2 11.8 %copy-start.8 = (bf16[8,384,128]{2,1,0:T(8,128)(2,1)S(1)}, bf16[8,384,128]{2,1,0:T(8,128)(2,1)}, u32[]{:S(2)}) copy-start(bf16[8,384,128]{2,1,0:T(8,128)(2,1)} %get-tuple-element.104) | copy-start | bytes 2359300
  259.4 41.1 %collective-permute-start.27 = (bf16[8,384,128]{2,1,0:T(8,128)(2,1)}, bf16[8,384,128]{2,1,0:T(8,128)(2,1)}, u32[]{:S(2)}, u32[]{:S(2)}) collective-permute-start(bf16[8,384,128]{2,1,0:T(8,128)(2,1)} %add.122), channel_id=1, source_target_pairs={{0,16},{16,0},{8,24},{24,8},{1,17},{17,1},{9,25},{25,9},{2,18},{18... | collective-permute-start | bytes 2359304 | tf_op jit(solution)/shard_map/ppermute | solution.py:762
  266.1 148.1 %reduce-scatter.11.cloned.1.call-start = ((), (), s32[]{:S(2)}) async-start(), calls=%async_computation.7 | async-start | bytes 884736 | tf_op jit(solution)/shard_map/reduce_scatter | solution.py:817
  266.2 30.9 %copy-start.18 = (f32[1,768]{1,0:T(1,128)S(1)}, f32[1,768]{1,0:T(1,128)}, u32[]{:S(2)}) copy-start(f32[1,768]{1,0:T(1,128)} %get-tuple-element.93) | copy-start | bytes 9220
  266.2 31.1 %copy-start.15 = (f32[1,1024]{1,0:T(1,128)S(1)}, f32[1,1024]{1,0:T(1,128)}, u32[]{:S(2)}) copy-start(f32[1,1024]{1,0:T(1,128)} %get-tuple-element.90) | copy-start | bytes 12292
  266.2 31.0 %copy-start.17 = (f32[1,1024]{1,0:T(1,128)S(1)}, f32[1,1024]{1,0:T(1,128)}, u32[]{:S(2)}) copy-start(f32[1,1024]{1,0:T(1,128)} %get-tuple-element.91) | copy-start | bytes 12292
  266.2 34.2 %copy-start.5 = (bf16[8,384,128]{2,1,0:T(8,128)(2,1)S(1)}, bf16[8,384,128]{2,1,0:T(8,128)(2,1)}, u32[]{:S(2)}) copy-start(bf16[8,384,128]{2,1,0:T(8,128)(2,1)} %get-tuple-element.102) | copy-start | bytes 2359300
  297.0 16.8 %collective-permute-start.8 = (bf16[8,432,128]{2,1,0:T(8,128)(2,1)}, bf16[8,432,128]{2,1,0:T(8,128)(2,1)S(1)}, u32[]{:S(2)}, u32[]{:S(2)}) collective-permute-start(bf16[8,432,128]{2,1,0:T(8,128)(2,1)} %get-tuple-element.82), channel_id=1, source_target_pairs={{0,8},{8,0},{16,24},{24,16},{1,9},{9,1},{17,25},{25,17},{2,10},{10... | collective-permute-start | bytes 2654216 | tf_op jit(solution)/shard_map/ppermute | solution.py:758
  299.4 43.4 %collective-permute-start.10 = (bf16[8,144,128]{2,1,0:T(8,128)(2,1)}, bf16[8,144,128]{2,1,0:T(8,128)(2,1)}, u32[]{:S(2)}, u32[]{:S(2)}) collective-permute-start(bf16[8,144,128]{2,1,0:T(8,128)(2,1)} %get-tuple-element.84), channel_id=1, source_target_pairs={{0,8},{8,0},{16,24},{24,16},{1,9},{9,1},{17,25},{25,17},{2,10},{10... | collective-permute-start | bytes 884744 | tf_op jit(solution)/shard_map/ppermute | solution.py:758
  299.9 19.4 %collective-permute-start.11 = (bf16[8,144,128]{2,1,0:T(8,128)(2,1)}, bf16[8,144,128]{2,1,0:T(8,128)(2,1)}, u32[]{:S(2)}, u32[]{:S(2)}) collective-permute-start(bf16[8,144,128]{2,1,0:T(8,128)(2,1)} %get-tuple-element.86), channel_id=1, source_target_pairs={{0,8},{8,0},{16,24},{24,16},{1,9},{9,1},{17,25},{25,17},{2,10},{10... | collective-permute-start | bytes 884744 | tf_op jit(solution)/shard_map/ppermute | solution.py:758
  299.9 44.1 %collective-permute-start.7 = (bf16[8,432,128]{2,1,0:T(8,128)(2,1)}, bf16[8,432,128]{2,1,0:T(8,128)(2,1)S(1)}, u32[]{:S(2)}, u32[]{:S(2)}) collective-permute-start(bf16[8,432,128]{2,1,0:T(8,128)(2,1)} %get-tuple-element.80), channel_id=1, source_target_pairs={{0,8},{8,0},{16,24},{24,16},{1,9},{9,1},{17,25},{25,17},{2,10},{10... | collective-permute-start | bytes 2654216 | tf_op jit(solution)/shard_map/ppermute | solution.py:758
  302.6 174.8 %reduce-scatter.5.cloned.1.call-start = ((), (), s32[]{:S(2)}) async-start(), calls=%async_computation.4 | async-start | bytes 1363968 | tf_op jit(solution)/shard_map/reduce_scatter | solution.py:817
  302.7 11.1 %copy-start.4 = (bf16[8,432,128]{2,1,0:T(8,128)(2,1)S(1)}, bf16[8,432,128]{2,1,0:T(8,128)(2,1)}, u32[]{:S(2)}) copy-start(bf16[8,432,128]{2,1,0:T(8,128)(2,1)} %get-tuple-element.81) | copy-start | bytes 2654212
  314.1 30.0 %copy-start.3 = (bf16[8,432,128]{2,1,0:T(8,128)(2,1)S(1)}, bf16[8,432,128]{2,1,0:T(8,128)(2,1)}, u32[]{:S(2)}) copy-start(bf16[8,432,128]{2,1,0:T(8,128)(2,1)} %get-tuple-element.79) | copy-start | bytes 2654212
  314.1 29.9 %collective-permute-start.9 = (bf16[8,432,128]{2,1,0:T(8,128)(2,1)S(1)}, bf16[8,432,128]{2,1,0:T(8,128)(2,1)S(1)}, u32[]{:S(2)}, u32[]{:S(2)}) collective-permute-start(bf16[8,432,128]{2,1,0:T(8,128)(2,1)S(1)} %add.108), channel_id=1, source_target_pairs={{0,16},{16,0},{8,24},{24,8},{1,17},{17,1},{9,25},{25,9},{2,18},{18... | collective-permute-start | bytes 2654216 | tf_op jit(solution)/shard_map/ppermute | solution.py:762
  321.1 21.7 %collective-permute-start.12 = (bf16[8,144,128]{2,1,0:T(8,128)(2,1)}, bf16[8,144,128]{2,1,0:T(8,128)(2,1)}, u32[]{:S(2)}, u32[]{:S(2)}) collective-permute-start(bf16[8,144,128]{2,1,0:T(8,128)(2,1)} %add.111), channel_id=1, source_target_pairs={{0,16},{16,0},{8,24},{24,8},{1,17},{17,1},{9,25},{25,9},{2,18},{18... | collective-permute-start | bytes 884744 | tf_op jit(solution)/shard_map/ppermute | solution.py:762
  332.8 1.2 collective-permute-start.13
  334.7 8.1 %collective-permute-start.14 = (bf16[8,9,128]{2,1,0:T(8,128)(2,1)S(1)}, bf16[8,9,128]{2,1,0:T(8,128)(2,1)S(1)}, u32[]{:S(2)}, u32[]{:S(2)}) collective-permute-start(bf16[8,9,128]{2,1,0:T(8,128)(2,1)S(1)} %copy_add_fusion), channel_id=1, source_target_pairs={{0,16},{16,0},{8,24},{24,8},{1,17},{17,1},{9,25},{25,9},{2,18},{18... | collective-permute-start | bytes 55304 | tf_op jit(solution)/shard_map/ppermute | solution.py:762
  415.1 7.1 %collective-permute-start.28 = (bf16[3,384,128]{2,1,0:T(8,128)(2,1)S(1)}, bf16[3,384,128]{2,1,0:T(8,128)(2,1)S(1)}, u32[]{:S(2)}, u32[]{:S(2)}) collective-permute-start(bf16[3,384,128]{2,1,0:T(8,128)(2,1)S(1)} %constant_dynamic-update-slice_fusion), channel_id=1, source_target_pairs={{0,16},{16,0},{8,24},{24,8},{1,17},{17,1},{9,25},{25,9},{2,18},{18... | collective-permute-start | bytes 884744 | tf_op jit(solution)/shard_map/ppermute | solution.py:762
  422.3 2.1 collective-permute-start.29
  478.9 4.2 collective-permute-start.17
  482.5 4.7 collective-permute-start.15
  483.1 5.0 %collective-permute-start.18 = (bf16[1,288,128]{2,1,0:T(8,128)(2,1)S(1)}, bf16[1,288,128]{2,1,0:T(8,128)(2,1)S(1)}, u32[]{:S(2)}, u32[]{:S(2)}) collective-permute-start(bf16[1,288,128]{2,1,0:T(8,128)(2,1)S(1)} %maximum_select_fusion.5), channel_id=1, source_target_pairs={{0,8},{8,0},{16,24},{24,16},{1,9},{9,1},{17,25},{25,17},{2,10},{10... | collective-permute-start | bytes 221192 | tf_op jit(solution)/shard_map/ppermute | solution.py:758
  487.4 1.6 collective-permute-start.16
  (16 other events, 45.8 us)
Sparse Core Ops, SparseCore 0:
  12.7 42.9 all-gather.8
  58.5 43.0 all-gather.10
  104.3 44.7 all-gather.6
  223.8 60.7 reduce-scatter.6
  288.1 61.4 reduce-scatter.8
  352.8 61.3 reduce-scatter.10
  417.9 59.4 reduce-scatter.4
